TPU v7x, 128 devices: a whole 4x4x4 slice. The times are simulated.
128 devices in a mesh: group: 8 (over x_hi, z), blk: 16 (over y, x_lo, core).
Axes of the slice: x: 4 (x_hi: 2, x_lo: 2; x = x_hi * 2 + x_lo), y: 4, z: 4, core: 2. Of those that a mesh axis runs over, the one named last changes fastest.
Arguments:
- picture_embedding_unscaled: float32 [98304, 1024], P(('group', 'blk')), may hold values from -0.5 to 0.5
- caption_tower_outputs: bfloat16 [98304, 1280], P(('group', 'blk')), may hold values from -6 to 6
- caption_mapping_matrix: bfloat16 [1280, 1024], replicated, may hold values from -0.15625 to 0.15625
- matching_caption_index: int32 [98304], P(('group', 'blk')), may hold values from 0 to 98303, as said below
- similarity_scaling: float32 [1], replicated, may hold values from 48 to 80
- score_offset: float32 [1], replicated, may hold values from -9.5 to -7.5
Outputs:
- grad_image: float32 [98304, 1024], P(('group', 'blk'))
- grad_proj: float32 [1280, 1024], replicated
Inputs may be any that keep to these rules, and one draw needn't show every extreme that they name: `matching_caption_index`: the positive of image row i of block (g, k) lies in one of the text blocks paired with that image block in the window: (g, k - s mod 16) for some s from 0 to 1, or (g - 1 mod 8, k - 1 mod 16).
All inputs are finite; a program needn't handle non-finite values.
Results may differ from a plain program's by a relative error of at most 0.0063.
Values may be sent and summed in bfloat16 or wider, within the bound.
A program may use at most 128 MiB of HBM per device.

v0:
```python
import jax
import jax.numpy as jnp
from jax import lax
from jax.sharding import PartitionSpec as P

STEPS = 1


epsilon = 1e-06


def shifted(value, axis, steps):
    count = lax.axis_size(axis)
    pairs = [(source, (source + steps) % count) for source in range(count)]
    return lax.ppermute(value, axis, pairs)


def unit_rows(values):
    scale = jnp.sqrt(jnp.sum(values * values, axis=-1, keepdims=True) + epsilon)
    return (values / scale, scale)


def pair_terms(
    image_unit, text_block, matching_caption_index, first_column, similarity_factor, logit_shift
):
    logits = (
        similarity_factor
        * lax.dot_general(
            image_unit, text_block, (((1,), (1,)), ((), ())), preferred_element_type=jnp.float32
        )
        + logit_shift
    )
    columns = first_column + lax.broadcasted_iota(jnp.int32, (1, text_block.shape[0]), 1)
    labels = jnp.where(matching_caption_index[:, None] == columns, 1.0, -1.0).astype(jnp.float32)
    weight = (-labels * jax.nn.sigmoid(-labels * logits)).astype(jnp.bfloat16)
    image_grad = similarity_factor * jnp.dot(weight, text_block, preferred_element_type=jnp.float32)
    text_grad = similarity_factor * lax.dot_general(
        weight, image_unit, (((0,), (0,)), ((), ())), preferred_element_type=jnp.float32
    )
    return (image_grad, text_grad)


def on_device(
    picture_embedding_unscaled,
    caption_tower_outputs,
    caption_mapping_matrix,
    matching_caption_index,
    similarity_scaling,
    score_offset,
):
    similarity_factor = similarity_scaling[0]
    logit_shift = score_offset[0]
    block_rows = picture_embedding_unscaled.shape[0]
    group_count = lax.axis_size("group")
    cycle_size = lax.axis_size("blk")
    group_index = lax.axis_index("group")
    cycle_index = lax.axis_index("blk")

    def holder_first_row(source_group, source_cycle):
        return (source_group % group_count * cycle_size + source_cycle % cycle_size) * block_rows

    image_unit32, image_scale = unit_rows(picture_embedding_unscaled)
    image_unit = image_unit32.astype(jnp.bfloat16)
    projected = jnp.dot(
        caption_tower_outputs, caption_mapping_matrix, preferred_element_type=jnp.float32
    )
    text_unit32, text_scale = unit_rows(projected)
    text_unit = text_unit32.astype(jnp.bfloat16)
    image_grad, own_grad = pair_terms(
        image_unit,
        text_unit,
        matching_caption_index,
        holder_first_row(group_index, cycle_index),
        similarity_factor,
        logit_shift,
    )
    moving = text_unit
    carried = own_grad
    moving = shifted(moving, "blk", 1)
    image_part, text_part = pair_terms(
        image_unit,
        moving,
        matching_caption_index,
        holder_first_row(group_index, cycle_index - 1),
        similarity_factor,
        logit_shift,
    )
    image_grad = image_grad + image_part
    carried = shifted(carried, "blk", 1) + text_part
    shifted_texts = shifted(moving, "group", 1)
    image_part, text_part = pair_terms(
        image_unit,
        shifted_texts,
        matching_caption_index,
        holder_first_row(group_index - 1, cycle_index - STEPS),
        similarity_factor,
        logit_shift,
    )
    image_grad = image_grad + image_part
    returned = shifted(text_part, "group", -1)
    text_grad = shifted(carried + returned, "blk", -STEPS)
    grad_image = (
        image_grad - image_unit32 * jnp.sum(image_unit32 * image_grad, axis=-1, keepdims=True)
    ) / image_scale
    grad_projected = (
        (text_grad - text_unit32 * jnp.sum(text_unit32 * text_grad, axis=-1, keepdims=True))
        / text_scale
    ).astype(jnp.bfloat16)
    head_terms = lax.dot_general(
        caption_tower_outputs,
        grad_projected,
        (((0,), (0,)), ((), ())),
        preferred_element_type=jnp.float32,
    )
    grad_proj = lax.psum(head_terms, ("group", "blk"))
    return (grad_image, grad_proj)


def solution(mesh):
    return jax.shard_map(
        on_device,
        mesh=mesh,
        in_specs=(
            P(("group", "blk"), None),
            P(("group", "blk"), None),
            P(),
            P(("group", "blk")),
            P(),
            P(),
        ),
        out_specs=(P(("group", "blk"), None), P()),
        check_vma=False,
    )
```

profile of v0, /device:TPU:1, one launch (start us, length us, event | category | flops | bytes accessed | tf_op | source)
XLA Modules:
  0.0 369.3 jit_solution(10106399722248772477)
XLA Ops:
  7.2 0.0 copy-start
  7.2 0.0 all-reduce.2.cloned.1.call-start
  7.2 1.7 copy-done
  8.9 3.8 %multiply_reduce_fusion.2 = (f32[768]{0:T(1024)S(1)}, f32[768,1024]{1,0:T(8,128)S(1)}) fusion(bf16[768,1280]{1,0:T(8,128)(2,1)} %param.7, bf16[1280,1024]{1,0:T(8,128)(2,1)S(1)} %copy-done), kind=kOutput, calls=%fused_computation.7 | convolution fusion | flops 2014838016 | bytes 7736320 | tf_op jit(solution)/shard_map/dot_general | solution.py:64
  12.7 0.0 copy-start.3
  12.8 0.0 copy-start.2
  12.8 1.6 fusion.3
  14.3 0.8 copy-done.3
  15.1 2.6 collective-permute-start
  19.1 0.0 copy-done.2
  19.1 0.3 multiply_reduce_fusion.3
  19.4 0.0 copy-start.11
  19.4 16.0 %collective-permute-done = bf16[768,1024]{1,0:T(8,128)(2,1)} collective-permute-done((bf16[768,1024]{1,0:T(8,128)(2,1)}, bf16[768,1024]{1,0:T(8,128)(2,1)}, u32[]{:S(2)}, u32[]{:S(2)}) %collective-permute-start) | collective-permute-done | bytes 1572896 | tf_op jit(solution)/shard_map/ppermute | solution.py:15
  35.4 1.6 collective-permute-start.1
  37.0 0.4 fusion.2
  37.4 0.0 copy-start.5
  37.5 0.0 copy-done.11
  37.5 3.9 %multiply_convert_fusion.2 = bf16[768,768]{1,0:T(8,128)(2,1)S(1)} fusion(bf16[768,1024]{1,0:T(8,128)(2,1)S(1)} %fusion.2, bf16[768,1024]{1,0:T(8,128)(2,1)} %fusion.3, f32[]{:T(128)} %bitcast.32, f32[]{:T(128)} %bitcast.26, s32[768]{0:T(1024)S(1)} %iota_add_fusion.2, s32[768]{0:T(1024)S(1)} %copy-done.11), kind=kOutput, calls=%fused_computation.11 | convolution fusion | flops 1214447616 | bytes 4331528 | tf_op jit(solution)/shard_map/dot_general | solution.py:28
  41.4 0.0 copy-start.12
  41.4 0.0 copy-done.5
  41.4 3.1 convolution_multiply_fusion.1
  44.5 0.0 copy-done.12
  44.5 2.8 collective-permute-start.2
  47.3 25.3 %collective-permute-done.1 = bf16[768,1024]{1,0:T(8,128)(2,1)} collective-permute-done((bf16[768,1024]{1,0:T(8,128)(2,1)}, bf16[768,1024]{1,0:T(8,128)(2,1)}, u32[]{:S(2)}, u32[]{:S(2)}) %collective-permute-start.1) | collective-permute-done | bytes 1572896 | tf_op jit(solution)/shard_map/ppermute | solution.py:15
  72.6 0.0 copy-start.6
  72.6 4.0 %multiply_convert_fusion = bf16[768,768]{1,0:T(8,128)(2,1)S(1)} fusion(bf16[768,1024]{1,0:T(8,128)(2,1)} %copy-done.5, bf16[768,1024]{1,0:T(8,128)(2,1)} %collective-permute-done.1, s32[768]{0:T(1024)S(1)} %iota_add_fusion, f32[]{:T(128)} %bitcast.33, f32[]{:T(128)} %bitcast.30, s32[768]{0:T(1024)S(1)} %copy-done.11), kind=kOutput, calls=%fused_computation.9 | convolution fusion | flops 1214447616 | bytes 4331528 | tf_op jit(solution)/shard_map/dot_general | solution.py:28
  76.5 0.0 copy-start.13
  76.5 0.0 copy-done.6
  76.6 3.1 convolution_multiply_fusion
  79.7 0.0 copy-done.13
  79.7 1.2 collective-permute-start.3
  80.9 0.0 copy-start.7
  80.9 4.0 %multiply_convert_fusion.1 = bf16[768,768]{1,0:T(8,128)(2,1)S(1)} fusion(bf16[768,1024]{1,0:T(8,128)(2,1)} %copy-done.5, bf16[768,1024]{1,0:T(8,128)(2,1)} %collective-permute-done, s32[768]{0:T(1024)S(1)} %iota_add_fusion.1, f32[]{:T(128)} %bitcast.34, f32[]{:T(128)} %bitcast.31, s32[768]{0:T(1024)S(1)} %copy-done.11), kind=kOutput, calls=%fused_computation.10 | convolution fusion | flops 1214447616 | bytes 4331528 | tf_op jit(solution)/shard_map/dot_general | solution.py:28
  84.9 0.0 copy-start.8
  84.9 0.0 collective-permute-done.2
  84.9 57.0 %collective-permute-done.3 = f32[768,1024]{1,0:T(8,128)} collective-permute-done((f32[768,1024]{1,0:T(8,128)}, f32[768,1024]{1,0:T(8,128)}, u32[]{:S(2)}, u32[]{:S(2)}) %collective-permute-start.3) | collective-permute-done | bytes 3145760 | tf_op jit(solution)/shard_map/ppermute | solution.py:15
  141.8 0.0 copy-done.7
  141.8 0.0 copy-start.4
  141.8 4.5 %add_add_fusion = f32[768,1024]{1,0:T(8,128)S(1)} fusion(f32[768,1024]{1,0:T(8,128)} %collective-permute-done.3, f32[768,1024]{1,0:T(8,128)} %collective-permute-done.2, bf16[768,768]{1,0:T(8,128)(2,1)S(1)} %multiply_convert_fusion.1, bf16[768,1024]{1,0:T(8,128)(2,1)S(1)} %copy-done.7, f32[]{:T(128)} %bitcast.28), kind=kOutput, calls=%fused_computation.4 | convolution fusion | flops 1210318848 | bytes 12189700 | tf_op jit(solution)/shard_map/dot_general | solution.py:37
  146.4 0.0 copy-done.8
  146.4 0.0 copy-start.10
  146.4 8.7 %collective-permute-start.4 = (f32[768,1024]{1,0:T(8,128)S(1)}, f32[768,1024]{1,0:T(8,128)S(1)}, u32[]{:S(2)}, u32[]{:S(2)}) collective-permute-start(f32[768,1024]{1,0:T(8,128)S(1)} %add_add_fusion), channel_id=1, source_target_pairs={{0,15},{1,0},{2,1},{3,2},{4,3},{5,4},{6,5},{7,6},{8,7},{9,8},{10,9... | collective-permute-start | bytes 9437192 | tf_op jit(solution)/shard_map/ppermute | solution.py:15
  155.1 38.5 %collective-permute-done.4 = f32[768,1024]{1,0:T(8,128)S(1)} collective-permute-done((f32[768,1024]{1,0:T(8,128)S(1)}, f32[768,1024]{1,0:T(8,128)S(1)}, u32[]{:S(2)}, u32[]{:S(2)}) %collective-permute-start.4) | collective-permute-done | bytes 3145760 | tf_op jit(solution)/shard_map/ppermute | solution.py:15
  193.7 0.0 copy-done.4
  193.7 0.5 multiply_reduce_fusion
  194.1 0.0 copy-done.10
  194.1 5.3 %convolution_bitcast_fusion = f32[1280,1024]{0,1:T(8,128)} fusion(bf16[768,1280]{1,0:T(8,128)(2,1)S(1)} %copy-done.10, f32[768,1024]{1,0:T(8,128)S(1)} %collective-permute-done.4, f32[768]{0:T(1024)S(1)} %multiply_reduce_fusion, f32[768]{0:T(1024)S(1)} %add_sqrt_fusion, f32[768,1024]{1,0:T(8,128)S(1)} %copy-done.4), kind=kOutput, calls=%fused_computation | convolution fusion | flops 2017198080 | bytes 13506560 | tf_op jit(solution)/shard_map/dot_general | solution.py:109
  199.4 0.0 all-reduce.2.cloned.1.call-update
  199.5 0.0 copy-start.9
  199.5 3.2 fusion.4
  202.7 0.0 copy-done.9
  202.7 0.0 copy-start.14
  202.7 2.9 fusion.5
  205.6 0.0 copy-done.14
  205.6 3.4 multiply_reduce_fusion.1
  209.1 2.2 subtract_divide_fusion
  211.3 145.1 %all-reduce.2.cloned.1.call-done = f32[1280,1024]{0,1:T(8,128)} async-done(((f32[1280,1024]{0,1:T(8,128)}), f32[1280,1024]{0,1:T(8,128)}) %all-reduce.2.cloned.1.call-update) | async-done | bytes 5242896 | tf_op jit(solution)/shard_map/psum | solution.py:115
  356.4 0.0 copy-start.1
  356.4 6.0 %copy.8 = f32[1280,1024]{1,0:T(8,128)} copy(f32[1280,1024]{0,1:T(8,128)} %all-reduce.2.cloned.1.call-done) | data formatting | bytes 10485760
  362.4 0.0 copy-done.1
  (5 shorter events, 0.0 us)
Async XLA Ops:
  7.2 1.7 copy-start
  7.2 349.2 %all-reduce.2.cloned.1.call-start = ((), (), s32[]{:S(2)}) async-start(), calls=%async_computation | async-start | bytes 10485760 | tf_op jit(solution)/shard_map/psum | solution.py:115
  12.7 2.4 copy-start.3
  12.8 6.3 %copy-start.2 = (f32[768,1024]{1,0:T(8,128)S(1)}, f32[768,1024]{1,0:T(8,128)}, u32[]{:S(2)}) copy-start(f32[768,1024]{1,0:T(8,128)} %param.6) | copy-start | bytes 9437188
  15.1 20.3 %collective-permute-start = (bf16[768,1024]{1,0:T(8,128)(2,1)}, bf16[768,1024]{1,0:T(8,128)(2,1)}, u32[]{:S(2)}, u32[]{:S(2)}) collective-permute-start(bf16[768,1024]{1,0:T(8,128)(2,1)} %fusion.3), channel_id=1, source_target_pairs={{0,1},{1,2},{2,3},{3,4},{4,5},{5,6},{6,7},{7,8},{8,9},{9,10},{10,1... | collective-permute-start | bytes 4718600 | tf_op jit(solution)/shard_map/ppermute | solution.py:15
  19.4 18.1 %copy-start.11 = (s32[768]{0:T(1024)S(1)}, s32[768]{0:T(1024)}, u32[]{:S(2)}) copy-start(s32[768]{0:T(1024)} %param.9) | copy-start | bytes 9220
  35.4 37.2 %collective-permute-start.1 = (bf16[768,1024]{1,0:T(8,128)(2,1)}, bf16[768,1024]{1,0:T(8,128)(2,1)}, u32[]{:S(2)}, u32[]{:S(2)}) collective-permute-start(bf16[768,1024]{1,0:T(8,128)(2,1)} %collective-permute-done), channel_id=1, source_target_pairs={{0,16},{16,32},{32,48},{48,64},{64,80},{80,96},{96,112},{112,0},{1... | collective-permute-start | bytes 4718600 | tf_op jit(solution)/shard_map/ppermute | solution.py:15
  37.4 4.0 %copy-start.5 = (bf16[768,1024]{1,0:T(8,128)(2,1)}, bf16[768,1024]{1,0:T(8,128)(2,1)S(1)}, u32[]{:S(2)}) copy-start(bf16[768,1024]{1,0:T(8,128)(2,1)S(1)} %fusion.2) | copy-start | bytes 4718596
  41.4 3.1 copy-start.12
  44.5 40.3 %collective-permute-start.2 = (f32[768,1024]{1,0:T(8,128)}, f32[768,1024]{1,0:T(8,128)}, u32[]{:S(2)}, u32[]{:S(2)}) collective-permute-start(f32[768,1024]{1,0:T(8,128)} %convolution_multiply_fusion.1), channel_id=1, source_target_pairs={{0,1},{1,2},{2,3},{3,4},{4,5},{5,6},{6,7},{7,8},{8,9},{9,10},{10,1... | collective-permute-start | bytes 9437192 | tf_op jit(solution)/shard_map/ppermute | solution.py:15
  72.6 4.0 %copy-start.6 = (bf16[768,1024]{1,0:T(8,128)(2,1)S(1)}, bf16[768,1024]{1,0:T(8,128)(2,1)}, u32[]{:S(2)}) copy-start(bf16[768,1024]{1,0:T(8,128)(2,1)} %copy-done.5) | copy-start | bytes 4718596
  76.5 3.1 copy-start.13
  79.7 62.2 %collective-permute-start.3 = (f32[768,1024]{1,0:T(8,128)}, f32[768,1024]{1,0:T(8,128)}, u32[]{:S(2)}, u32[]{:S(2)}) collective-permute-start(f32[768,1024]{1,0:T(8,128)} %convolution_multiply_fusion), channel_id=1, source_target_pairs={{0,112},{16,0},{32,16},{48,32},{64,48},{80,64},{96,80},{112,96},{1... | collective-permute-start | bytes 9437192 | tf_op jit(solution)/shard_map/ppermute | solution.py:15
  80.9 61.0 %copy-start.7 = (bf16[768,1024]{1,0:T(8,128)(2,1)S(1)}, bf16[768,1024]{1,0:T(8,128)(2,1)}, u32[]{:S(2)}) copy-start(bf16[768,1024]{1,0:T(8,128)(2,1)} %copy-done.5) | copy-start | bytes 4718596
  84.9 61.5 %copy-start.8 = (bf16[768,768]{1,0:T(8,128)(2,1)}, bf16[768,768]{1,0:T(8,128)(2,1)S(1)}, u32[]{:S(2)}) copy-start(bf16[768,768]{1,0:T(8,128)(2,1)S(1)} %multiply_convert_fusion.1) | copy-start | bytes 3538948
  141.8 51.8 %copy-start.4 = (f32[768,1024]{1,0:T(8,128)S(1)}, f32[768,1024]{1,0:T(8,128)}, u32[]{:S(2)}) copy-start(f32[768,1024]{1,0:T(8,128)} %copy-done.3) | copy-start | bytes 9437188
  146.4 47.8 %copy-start.10 = (bf16[768,1280]{1,0:T(8,128)(2,1)S(1)}, bf16[768,1280]{1,0:T(8,128)(2,1)}, u32[]{:S(2)}) copy-start(bf16[768,1280]{1,0:T(8,128)(2,1)} %param.7) | copy-start | bytes 5898244
  146.4 47.3 %collective-permute-start.4 = (f32[768,1024]{1,0:T(8,128)S(1)}, f32[768,1024]{1,0:T(8,128)S(1)}, u32[]{:S(2)}, u32[]{:S(2)}) collective-permute-start(f32[768,1024]{1,0:T(8,128)S(1)} %add_add_fusion), channel_id=1, source_target_pairs={{0,15},{1,0},{2,1},{3,2},{4,3},{5,4},{6,5},{7,6},{8,7},{9,8},{10,9... | collective-permute-start | bytes 9437192 | tf_op jit(solution)/shard_map/ppermute | solution.py:15
  199.5 3.3 copy-start.9
  202.7 2.9 copy-start.14
  356.4 6.0 %copy-start.1 = (bf16[1280,1024]{1,0:T(8,128)(2,1)S(1)}, bf16[1280,1024]{1,0:T(8,128)(2,1)}, u32[]{:S(2)}) copy-start(bf16[1280,1024]{1,0:T(8,128)(2,1)} %param.8) | copy-start | bytes 7864324
Sparse Core Ops, SparseCore 0:
  199.6 156.7 all-reduce.1
where the time goes:
time: 370 us; the launch traced here: 369 us
  waiting for transfers between devices  282 us (76%)
  matrix products  41.3 us (11%)
  starting transfers between devices  17 us (5%)
  between operations  15.6 us (4%)
  local copies, waits for them, and re-layouts  8.59 us (2%)
  other arithmetic  4.96 us (1%)
    psum x1, waiting for transfers between devices, on_device(): grad_proj = lax.psum(head_terms, ('group', 'blk'))  145 us
    ppermute x5, waiting for transfers between devices, shifted(): return lax.ppermute(value, axis, pairs)  137 us
    ppermute x5, starting transfers between devices, shifted(): return lax.ppermute(value, axis, pairs)  16.9 us
    dot_general x3, matrix products, pair_terms(): lax.dot_general(image_unit, text_block, (((1,), (1,)), ((), ())), preferr...  11.9 us
    dot_general x3, matrix products, pair_terms(): lax.dot_general(weight, image_unit, (((0,), (0,)), ((), ())), preferred_e...  10.7 us
    dot_general x3, matrix products, pair_terms(): jnp.dot(weight, text_block, preferred_element_type=jnp.float32)  9.57 us
    unnamed x31, local copies, waits for them, and re-layouts  8.59 us
  transfers between devices with their start and end apart: 6, of which 5 were waited for; matrix products, arithmetic and copies ran while one was open for 8% of the time, Pallas kernels for 0%

commit v1 on v0

v1 whole, which is shorter than its diff:
```python
import jax
import jax.numpy as jnp
from jax import lax
from jax.experimental import pallas as pl
from jax.experimental.pallas import tpu as pltpu
from jax.sharding import PartitionSpec as P

EPS = 1e-06
ROWS = 768
E = 1024
FT = 1280
SEND = 128
SENDS = ROWS // SEND
TILE = 256
TILES = ROWS // TILE
HALF = E // 2
MESH = pl.DeviceIdType.MESH
BF16 = jnp.bfloat16
F32 = jnp.float32

PARTS = ((0, 32, "yxz"), (512, 32, "zyx"), (1024, 16, "xzy"))


def start_copy(src, dst, send, recv, device):
    pltpu.make_async_remote_copy(
        src_ref=src, dst_ref=dst, send_sem=send, recv_sem=recv, device_id=device, device_id_type=MESH
    ).start()


def wait_sent(src, send):
    pltpu.make_async_copy(src, src, send).wait()


def wait_got(dst, recv):
    pltpu.make_async_copy(dst, dst, recv).wait()


def kernel(
    scale_ref, bias_ref, index_ref, pic_hbm, cap_hbm, head_hbm,
    gi_ref, out_ref,
    pic, cap, head, iu, tu, tu32, trs, cap_t, i2, i3, t2, t3, idx, idx2, idx3, idx_col,
    w, g_text, g_image, gp, hs, r0, d, r1a, r1b, r1c, e_a, e_b, e_c, r2a, r2b, r2c, f_a, f_b, f_c, r3a, r3b, r3c,
    load_sem, is2, ir2, is3, ir3, is3r, ts2, tr2, ts3, tr3, ts3r, xs2, xr2, xs3, xr3,
    s0s, s0r, rs_s, rs_r, ag_s, ag_r, a0s, a0r,
):
    g = lax.axis_index("group")
    k = lax.axis_index("blk")
    z = g % 4
    y = k // 4
    x = (g // 4) * 2 + (k // 2) % 2
    core = k % 2
    odd = core == 1
    even = core == 0
    place = {"x": x, "y": y, "z": z}

    def device(xx, yy, zz, cc):
        return ((xx // 2) * 4 + zz, yy * 4 + (xx % 2) * 2 + cc)

    def on_axis(axis, d):
        p = dict(place)
        p[axis] = (p[axis] + d) % 4
        return device(p["x"], p["y"], p["z"], core)

    def shift(dg, dk):
        return ((g + dg + 8) % 8, (k + dk + 16) % 16)

    other_core = device(x, y, z, 1 - core)

    loads = []
    for c in range(SENDS):
        loads.append(pltpu.make_async_copy(pic_hbm.at[pl.ds(c * SEND, SEND)], pic.at[pl.ds(c * SEND, SEND)], load_sem.at[c]))
    loads.append(pltpu.make_async_copy(cap_hbm, cap, load_sem.at[SENDS]))
    loads.append(pltpu.make_async_copy(head_hbm, head, load_sem.at[SENDS + 1]))
    for load in loads:
        load.start()

    barrier = pltpu.get_barrier_semaphore()
    partners = [shift(0, 1), shift(0, -1), shift(1, 0), shift(-1, 0), shift(1, 1), shift(-1, -1), other_core]
    for axis in "xyz":
        for step in (1, 2, 3):
            partners.append(on_axis(axis, step))
    for p in partners:
        pl.semaphore_signal(barrier, inc=1, device_id=p, device_id_type=MESH)

    scale = scale_ref[0]
    bias = bias_ref[0]

    idx[...] = jnp.broadcast_to(index_ref[...], (8, ROWS))

    def normalize_image(c, _):
        r = pl.ds(pl.multiple_of(c * SEND, SEND), SEND)
        pltpu.make_async_copy(pic.at[r], pic.at[r], load_sem.at[c]).wait()
        v = pic[r, :]
        inv = lax.rsqrt(jnp.sum(v * v, axis=1, keepdims=True) + EPS)
        iu[r, :] = (v * inv).astype(BF16)
        return 0

    lax.fori_loop(0, SENDS, normalize_image, 0)
    pl.semaphore_wait(barrier, len(partners))

    direct_image = jnp.logical_or(odd, z == 0)
    direct_text = jnp.logical_or(even, z == 3)
    down = shift(0, -1)
    cross_down = shift(-1, -1)
    start_copy(idx, idx2, xs2, xr2, down)
    start_copy(idx, idx3, xs3, xr3, cross_down)

    def send_images(c, _):
        r = pl.ds(pl.multiple_of(c * SEND, SEND), SEND)
        start_copy(iu.at[r], i2.at[r], is2.at[c], ir2.at[c], down)

        @pl.when(direct_image)
        def _():
            start_copy(iu.at[r], i3.at[r], is3.at[c], ir3.at[c], cross_down)

        return 0

    lax.fori_loop(0, SENDS, send_images, 0)

    loads[SENDS].wait()
    loads[SENDS + 1].wait()

    def project(n, _):
        cols = pl.ds(pl.multiple_of(n * TILE, TILE), TILE)
        tu32[:, cols] = jnp.dot(cap[...], head[:, cols], preferred_element_type=F32)
        return 0

    lax.fori_loop(0, E // TILE, project, 0)

    def normalize_text(c, _):
        r = pl.ds(pl.multiple_of(c * SEND, SEND), SEND)
        v = tu32[r, :]
        inv = lax.rsqrt(jnp.sum(v * v, axis=1, keepdims=True) + EPS)
        u = v * inv
        tu32[r, :] = u
        tu[r, :] = u.astype(BF16)
        trs[r, :] = jnp.broadcast_to(inv, (SEND, 128))
        return 0

    lax.fori_loop(0, SENDS, normalize_text, 0)
    up = shift(0, 1)
    cross_up = shift(1, 1)

    def send_texts(c, _):
        r = pl.ds(pl.multiple_of(c * SEND, SEND), SEND)
        start_copy(tu.at[r], t2.at[r], ts2.at[c], tr2.at[c], up)

        @pl.when(direct_text)
        def _():
            start_copy(tu.at[r], t3.at[r], ts3.at[c], tr3.at[c], cross_up)

        return 0

    lax.fori_loop(0, SENDS, send_texts, 0)

    for c in range(ROWS // 128):
        row = jnp.broadcast_to(index_ref[0:1, pl.ds(c * 128, 128)], (128, 128))
        idx_col[pl.ds(c * 128, 128), :] = row.T

    own_first = (g * 16 + k) * ROWS

    def weights(logits, match):
        v = logits * scale + bias
        v = jnp.where(match, -v, v)
        s = 1.0 / (1.0 + jnp.exp(-v))
        return jnp.where(match, -s, s).astype(BF16)

    def text_logits(c, images, index):
        r = pl.ds(pl.multiple_of(c * TILE, TILE), TILE)
        logits = lax.dot_general(tu[...], images[r, :], (((1,), (1,)), ((), ())), preferred_element_type=F32)
        match = (index[0:1, r] - own_first) == lax.broadcasted_iota(jnp.int32, (ROWS, TILE), 0)
        w[:, r] = weights(logits, match)

    def image_logits(c, texts, first):
        r = pl.ds(pl.multiple_of(c * TILE, TILE), TILE)
        logits = lax.dot_general(iu[...], texts[r, :], (((1,), (1,)), ((), ())), preferred_element_type=F32)
        column = idx_col[...] - (first + c * TILE)
        column = jnp.concatenate([column, column - 128], axis=1)
        match = column == (lax.broadcasted_iota(jnp.int32, (ROWS, TILE), 1) % 128)
        w[:, r] = weights(logits, match)

    def add_grad(total, block, first):
        def step(n, _):
            cols = pl.ds(pl.multiple_of(n * TILE, TILE), TILE)
            term = jnp.dot(w[...], block[:, cols], preferred_element_type=F32)
            total[:, cols] = term if first else total[:, cols] + term
            return 0

        lax.fori_loop(0, E // TILE, step, 0)

    def text_side(images, index, first, before):
        def step(c, _):
            before(c)
            text_logits(c, images, index)
            return 0

        lax.fori_loop(0, TILES, step, 0)
        add_grad(g_text, images, first)

    def image_side(texts, first_row, first, before):
        def step(c, _):
            before(c)
            image_logits(c, texts, first_row)
            return 0

        lax.fori_loop(0, TILES, step, 0)
        add_grad(g_image, texts, first)

    def nothing(c):
        pass

    per = TILE // SEND

    def got(buffer, sems, forward):
        def before(c):
            for i in range(per):
                m = c * per + i
                r = pl.ds(pl.multiple_of(m * SEND, SEND), SEND)
                wait_got(buffer.at[r], sems.at[m])
                forward(m, r)

        return before

    def no_forward(m, r):
        pass

    forward_image = jnp.logical_and(odd, z != 0)
    forward_text = jnp.logical_and(even, z != 3)

    def pass_image(m, r):
        @pl.when(forward_image)
        def _():
            start_copy(i2.at[r], i3.at[r], is3r.at[m], ir3.at[m], shift(-1, 0))

    def pass_text(m, r):
        @pl.when(forward_text)
        def _():
            start_copy(t2.at[r], t3.at[r], ts3r.at[m], tr3.at[m], shift(1, 0))

    text_side(iu, idx, True, nothing)
    image_side(tu, own_first, True, nothing)

    def turn(n, _):
        cols = pl.ds(pl.multiple_of(n * TILE, TILE), TILE)
        for m in range(TILES):
            cap_t[cols, pl.ds(m * TILE, TILE)] = cap[pl.ds(m * TILE, TILE), cols].T
        return 0

    lax.fori_loop(0, FT // TILE, turn, 0)

    wait_got(idx2, xr2)
    text_side(i2, idx2, False, got(i2, ir2, pass_image))
    before_t2 = got(t2, tr2, pass_text)

    def step_t2(c, _):
        before_t2(c)
        return 0

    lax.fori_loop(0, TILES, step_t2, 0)
    wait_got(idx3, xr3)
    text_side(i3, idx3, False, got(i3, ir3, no_forward))

    def finish_text(c, _):
        r = pl.ds(pl.multiple_of(c * SEND, SEND), SEND)
        u = tu32[r, :]
        v = g_text[r, :] * scale
        dot = jnp.sum(u * v, axis=1, keepdims=True)
        gp[r, :] = ((v - u * dot) * trs[r, 0:1]).astype(BF16)
        return 0

    lax.fori_loop(0, SENDS, finish_text, 0)

    r1 = (r1a, r1b, r1c)
    e_ = (e_a, e_b, e_c)
    r2 = (r2a, r2b, r2c)
    f_ = (f_a, f_b, f_c)
    r3 = (r3a, r3b, r3c)
    mine = pl.multiple_of(core * HALF, HALF)
    theirs = pl.multiple_of((1 - core) * HALF, HALF)

    def span(p):
        base, own, _ = PARTS[p]
        return pl.ds(base, 16 * own)

    for p in range(3):
        rows = span(p)
        for n in range(HALF // TILE):
            hs[rows, pl.ds(n * TILE, TILE)] = jnp.dot(
                cap_t[rows, :], gp[:, pl.ds(pl.multiple_of(theirs + n * TILE, TILE), TILE)], preferred_element_type=F32
            ).astype(BF16)
        start_copy(hs.at[rows], r0.at[rows], s0s.at[p], s0r.at[p], other_core)

    for p in range(3):
        base, own, order = PARTS[p]
        rows = span(p)
        for n in range(HALF // TILE):
            term = jnp.dot(
                cap_t[rows, :], gp[:, pl.ds(pl.multiple_of(mine + n * TILE, TILE), TILE)], preferred_element_type=F32
            )
            if n == 0:
                wait_got(r0.at[rows], s0r.at[p])
            cols = pl.ds(n * TILE, TILE)
            d[rows, cols] = (term + r0[rows, cols].astype(F32)).astype(BF16)
        i = place[order[0]]
        for s in (1, 2, 3):
            j = (i + s) % 4
            start_copy(
                d.at[pl.ds(pl.multiple_of(base + j * 4 * own, 16), 4 * own)],
                r1[p].at[s - 1], rs_s.at[p, 0, s - 1], rs_r.at[p, 0, s - 1], on_axis(order[0], s),
            )

    def total(own, parts):
        v = own.astype(F32)
        for s in range(3):
            v = v + parts[s].astype(F32)
        return v.astype(BF16)

    image_side(t2, (g * 16 + (k + 15) % 16) * ROWS, False, nothing)

    for p in range(3):
        base, own, order = PARTS[p]
        for s in range(3):
            wait_got(r1[p].at[s], rs_r.at[p, 0, s])
        i = place[order[0]]
        e_[p][...] = total(d[pl.ds(pl.multiple_of(base + i * 4 * own, 16), 4 * own), :], [r1[p][s] for s in range(3)])
        i = place[order[1]]
        for s in (1, 2, 3):
            j = (i + s) % 4
            start_copy(
                e_[p].at[pl.ds(pl.multiple_of(j * own, 16), own)],
                r2[p].at[s - 1], rs_s.at[p, 1, s - 1], rs_r.at[p, 1, s - 1], on_axis(order[1], s),
            )
    for p in range(3):
        base, own, order = PARTS[p]
        for s in range(3):
            wait_got(r2[p].at[s], rs_r.at[p, 1, s])
        i = place[order[1]]
        f_[p][...] = total(e_[p][pl.ds(pl.multiple_of(i * own, 16), own), :], [r2[p][s] for s in range(3)])
        i = place[order[2]]
        for s in (1, 2, 3):
            j = (i + s) % 4
            start_copy(
                f_[p].at[:, pl.ds(pl.multiple_of(j * 128, 128), 128)],
                r3[p].at[s - 1], rs_s.at[p, 2, s - 1], rs_r.at[p, 2, s - 1], on_axis(order[2], s),
            )

    def block(p, a, b, c):
        base, own, _ = PARTS[p]
        if a is None:
            rows = pl.ds(base, 16 * own)
        elif b is None:
            rows = pl.ds(pl.multiple_of(base + a * 4 * own, 16), 4 * own)
        else:
            rows = pl.ds(pl.multiple_of(base + (a * 4 + b) * own, 16), own)
        if c is None:
            cols = pl.ds(mine, HALF)
        else:
            cols = pl.ds(pl.multiple_of(mine + c * 128, 128), 128)
        return rows, cols

    def gather(p, stage, rows, cols):
        axis = PARTS[p][2][stage]
        for s in (1, 2, 3):
            ref = out_ref.at[rows, cols]
            start_copy(ref, ref, ag_s.at[p, stage, s - 1], ag_r.at[p, stage, s - 1], on_axis(axis, s))

    def seat(p):
        order = PARTS[p][2]
        return [place[a] for a in order]

    for p in range(3):
        a, b, c = seat(p)
        for s in range(3):
            wait_got(r3[p].at[s], rs_r.at[p, 2, s])
        rows, cols = block(p, a, b, c)
        out_ref[rows, cols] = total(f_[p][:, pl.ds(pl.multiple_of(c * 128, 128), 128)], [r3[p][s] for s in range(3)])
        gather(p, 2, rows, cols)
    for p in range(3):
        a, b, c = seat(p)
        for s in (1, 2, 3):
            wait_got(out_ref.at[block(p, a, b, (c - s + 4) % 4)], ag_r.at[p, 2, s - 1])
        gather(p, 1, *block(p, a, b, None))
    for p in range(3):
        a, b, c = seat(p)
        for s in (1, 2, 3):
            wait_got(out_ref.at[block(p, a, (b - s + 4) % 4, None)], ag_r.at[p, 1, s - 1])
        gather(p, 0, *block(p, a, None, None))
        ref = out_ref.at[block(p, a, None, None)]
        start_copy(ref, ref, a0s.at[p, 0], a0r.at[p, 0], other_core)

    image_side(t3, (((g + 7) % 8) * 16 + (k + 15) % 16) * ROWS, False, got(t3, tr3, no_forward))

    def finish_image(c, _):
        r = pl.ds(pl.multiple_of(c * SEND, SEND), SEND)
        u = pic[r, :]
        inv = lax.rsqrt(jnp.sum(u * u, axis=1, keepdims=True) + EPS)
        u = u * inv
        v = g_image[r, :] * scale
        dot = jnp.sum(u * v, axis=1, keepdims=True)
        gi_ref[r, :] = ((v - u * dot) * inv).astype(BF16)
        return 0

    lax.fori_loop(0, SENDS, finish_image, 0)

    for p in range(3):
        a, b, c = seat(p)
        for s in (1, 2, 3):
            ref = out_ref.at[block(p, (a - s + 4) % 4, None, None)]
            wait_got(ref, ag_r.at[p, 0, s - 1])
            start_copy(ref, ref, a0s.at[p, s], a0r.at[p, s], other_core)
    for p in range(3):
        base, own, _ = PARTS[p]
        a, b, c = seat(p)
        for s in range(4):
            rows = pl.ds(pl.multiple_of(base + ((a - s + 4) % 4) * 4 * own, 16), 4 * own)
            wait_got(out_ref.at[rows, pl.ds(theirs, HALF)], a0r.at[p, s])

    wait_sent(idx, xs2)
    wait_sent(idx, xs3)

    def drain(c, _):
        r = pl.ds(pl.multiple_of(c * SEND, SEND), SEND)
        wait_sent(iu.at[r], is2.at[c])
        wait_sent(tu.at[r], ts2.at[c])

        @pl.when(direct_image)
        def _():
            wait_sent(iu.at[r], is3.at[c])

        @pl.when(direct_text)
        def _():
            wait_sent(tu.at[r], ts3.at[c])

        @pl.when(forward_image)
        def _():
            wait_sent(i2.at[r], is3r.at[c])

        @pl.when(forward_text)
        def _():
            wait_sent(t2.at[r], ts3r.at[c])

        return 0

    lax.fori_loop(0, SENDS, drain, 0)
    for p in range(3):
        base, own, _ = PARTS[p]
        a, b, c = seat(p)
        wait_sent(hs.at[span(p)], s0s.at[p])
        for s in range(3):
            wait_sent(r1[p].at[s], rs_s.at[p, 0, s])
            wait_sent(r2[p].at[s], rs_s.at[p, 1, s])
            wait_sent(r3[p].at[s], rs_s.at[p, 2, s])
            wait_sent(out_ref.at[block(p, a, b, c)], ag_s.at[p, 2, s])
            wait_sent(out_ref.at[block(p, a, b, None)], ag_s.at[p, 1, s])
            wait_sent(out_ref.at[block(p, a, None, None)], ag_s.at[p, 0, s])
        for s in range(4):
            wait_sent(out_ref.at[block(p, (a - s + 4) % 4, None, None)], a0s.at[p, s])


def scratch():
    vmem = pltpu.VMEM
    dma = pltpu.SemaphoreType.DMA
    block = vmem((ROWS, E), BF16)
    wide = vmem((ROWS, E), F32)
    index = vmem((8, ROWS), jnp.int32)
    owns = [own for _, own, _ in PARTS]
    return [
        wide, vmem((ROWS, FT), BF16), vmem((FT, E), BF16), block, block, wide, vmem((ROWS, 128), F32), vmem((FT, ROWS), BF16),
        block, block, block, block, index, index, index, vmem((ROWS, 128), jnp.int32),
        vmem((ROWS, ROWS), BF16), wide, wide, block, vmem((FT, HALF), BF16), vmem((FT, HALF), BF16), vmem((FT, HALF), BF16),
        *[vmem((3, 4 * own, HALF), BF16) for own in owns],
        *[vmem((4 * own, HALF), BF16) for own in owns],
        *[vmem((3, own, HALF), BF16) for own in owns],
        *[vmem((own, HALF), BF16) for own in owns],
        *[vmem((3, own, 128), BF16) for own in owns],
        dma((SENDS + 2,)),
        *[dma((SENDS,)) for _ in range(10)],
        dma, dma, dma, dma,
        dma((3,)), dma((3,)), dma((3, 3, 3)), dma((3, 3, 3)), dma((3, 3, 3)), dma((3, 3, 3)), dma((3, 4)), dma((3, 4)),
    ]


def on_device(
    picture_embedding_unscaled,
    caption_tower_outputs,
    caption_mapping_matrix,
    matching_caption_index,
    similarity_scaling,
    score_offset,
):
    smem = pl.BlockSpec(memory_space=pltpu.SMEM)
    vmem = pl.BlockSpec(memory_space=pltpu.VMEM)
    anywhere = pl.BlockSpec(memory_space=pl.ANY)
    grad_image, grad_proj = pl.pallas_call(
        kernel,
        out_shape=(jax.ShapeDtypeStruct((ROWS, E), BF16), jax.ShapeDtypeStruct((FT, E), BF16)),
        in_specs=[smem, smem, vmem, anywhere, anywhere, anywhere],
        out_specs=(vmem, vmem),
        scratch_shapes=scratch(),
        compiler_params=pltpu.CompilerParams(
            collective_id=0, has_side_effects=True, vmem_limit_bytes=52 * 1024 * 1024
        ),
    )(
        similarity_scaling, score_offset, matching_caption_index.reshape(1, ROWS),
        picture_embedding_unscaled, caption_tower_outputs, caption_mapping_matrix,
    )
    return grad_image.astype(F32), grad_proj.astype(F32)


def solution(mesh):
    return jax.shard_map(
        on_device,
        mesh=mesh,
        in_specs=(
            P(("group", "blk"), None),
            P(("group", "blk"), None),
            P(),
            P(("group", "blk")),
            P(),
            P(),
        ),
        out_specs=(P(("group", "blk"), None), P()),
        check_vma=False,
    )
```

time: 370 us -> 117 us (0.32)
  waiting for transfers between devices: 282 us -> 0 us
  Pallas kernels: 0 us -> 108 us
  matrix products: 41.3 us -> 0 us
  starting transfers between devices: 17 us -> 0 us
  between operations: 15.6 us -> 1.94 us
  local copies, waits for them, and re-layouts: 8.59 us -> 0.69 us
    psum x1 -> x0, waiting for transfers between devices: 145 us -> none  [on_device(): grad_proj = lax.psum(head_terms, ('group', 'blk'))]
    ppermute x5 -> x0, waiting for transfers between devices: 137 us -> none  [shifted(): return lax.ppermute(value, axis, pairs)]
    pallas_call x0 -> x1, Pallas kernels: none -> 108 us  [on_device(): pl.pallas_call(kernel, out_shape=(jax.ShapeDtypeStruct((ROWS, E), BF16),...]
    dot_general x11 -> x0, matrix products: 41.3 us -> none  [the longest x3 11.9 us: pair_terms(): lax.dot_general(image_unit, text_block, (((1,), (1,)), ((), ())), preferr...]
    ppermute x5 -> x0, starting transfers between devices: 16.9 us -> none  [shifted(): return lax.ppermute(value, axis, pairs)]
    unnamed x31 -> x0, local copies, waits for them, and re-layouts: 8.59 us -> none
    convert_element_type x2, other arithmetic: 1.96 us -> 6.82 us  [on_device(): return (grad_image.astype(F32), grad_proj.astype(F32))]
  transfers between devices with their start and end apart: 6 -> 0, of which waited for: 5 -> 0; matrix products, arithmetic and copies ran while one was open for 8% -> 0% of each run, Pallas kernels for 0% -> 0%
where the time goes in v1:
time: 117 us
  Pallas kernels  108 us (92%)
  other arithmetic  6.82 us (6%)
  between operations  1.94 us (2%)
    pallas_call x1, Pallas kernels, on_device(): pl.pallas_call(kernel, out_shape=(jax.ShapeDtypeStruct((ROWS, E), BF16),...  108 us
    convert_element_type x2, other arithmetic, on_device(): return (grad_image.astype(F32), grad_proj.astype(F32))  6.82 us

profile of v1, /device:TPU:1, one launch (start us, length us, event | category | flops | bytes accessed | tf_op | source)
XLA Modules:
  0.0 117.3 jit_solution(1315716223138353210)
XLA Ops:
  0.6 0.7 reshape.7.index_ref
  2.6 107.8 %shard_map.77 = (bf16[768,1024]{1,0:T(8,128)(2,1)S(1)}, bf16[1280,1024]{1,0:T(8,128)(2,1)}) custom-call(f32[1]{0:T(128)S(6)} %copy.8.scale_ref, f32[1]{0:T(128)S(6)} %copy.9.bias_ref, s32[1,768]{1,0:T(1,128)S(1)} %reshape.7.index_ref, f32[768,1024]{1,0:T(8,128)} %pic_hbm.1, bf16[768,1280]{1,0:T(8,128)(2,1)} %cap_hbm.1, bf16[1280,1024]{1,0:T(8,128)(2,1)} %head_hbm.1), custom_call_target="tpu_custom_call" | custom-call | tf_op jit(solution)/shard_map/pallas_call | solution.py:494
  110.4 4.7 %convert_element_type.7 = f32[1280,1024]{1,0:T(8,128)} convert(bf16[1280,1024]{1,0:T(8,128)(2,1)} %get-tuple-element.5) | non-fusion elementwise | flops 1310720 | bytes 7864320 | tf_op jit(solution)/shard_map/convert_element_type | solution.py:507
  115.2 2.1 %convert_element_type.6 = f32[768,1024]{1,0:T(8,128)} convert(bf16[768,1024]{1,0:T(8,128)(2,1)S(1)} %get-tuple-element.4) | non-fusion elementwise | flops 786432 | bytes 4718592 | tf_op jit(solution)/shard_map/convert_element_type | solution.py:507

commit v2 on v1

--- a/solution.py
+++ b/solution.py
@@ -18,7 +18,7 @@
 BF16 = jnp.bfloat16
 F32 = jnp.float32
 
-PARTS = ((0, 32, "yxz"), (512, 32, "zyx"), (1024, 16, "xzy"))
+PARTS = ((0, 32, "yzx"), (512, 32, "zyx"), (1024, 16, "xyz"))
 
 
 def start_copy(src, dst, send, recv, device):
@@ -36,11 +36,11 @@
 
 
 def kernel(
-    scale_ref, bias_ref, index_ref, pic_hbm, cap_hbm, head_hbm,
+    scale_hbm, bias_hbm, index_hbm, pic_hbm, cap_hbm, head_hbm,
     gi_ref, out_ref,
-    pic, cap, head, iu, tu, tu32, trs, cap_t, i2, i3, t2, t3, idx, idx2, idx3, idx_col,
+    scale_ref, bias_ref, index_ref, pic, cap, head, iu, tu, tu32, trs, cap_t, images, t2, t3, idx, far_idx, idx_col,
     w, g_text, g_image, gp, hs, r0, d, r1a, r1b, r1c, e_a, e_b, e_c, r2a, r2b, r2c, f_a, f_b, f_c, r3a, r3b, r3c,
-    load_sem, is2, ir2, is3, ir3, is3r, ts2, tr2, ts3, tr3, ts3r, xs2, xr2, xs3, xr3,
+    load_sem, is2, is3, is3r, images_got, ts2, tr2, ts3, tr3, ts3r, xs2, xs3, far_idx_got,
     s0s, s0r, rs_s, rs_r, ag_s, ag_r, a0s, a0r,
 ):
     g = lax.axis_index("group")
@@ -71,6 +71,9 @@
         loads.append(pltpu.make_async_copy(pic_hbm.at[pl.ds(c * SEND, SEND)], pic.at[pl.ds(c * SEND, SEND)], load_sem.at[c]))
     loads.append(pltpu.make_async_copy(cap_hbm, cap, load_sem.at[SENDS]))
     loads.append(pltpu.make_async_copy(head_hbm, head, load_sem.at[SENDS + 1]))
+    loads.append(pltpu.make_async_copy(index_hbm, index_ref, load_sem.at[SENDS + 2]))
+    loads.append(pltpu.make_async_copy(scale_hbm, scale_ref, load_sem.at[SENDS + 3]))
+    loads.append(pltpu.make_async_copy(bias_hbm, bias_ref, load_sem.at[SENDS + 4]))
     for load in loads:
         load.start()
 
@@ -82,10 +85,9 @@
     for p in partners:
         pl.semaphore_signal(barrier, inc=1, device_id=p, device_id_type=MESH)
 
-    scale = scale_ref[0]
-    bias = bias_ref[0]
-
-    idx[...] = jnp.broadcast_to(index_ref[...], (8, ROWS))
+    direct_image = jnp.logical_or(odd, z == 0)
+    down = shift(0, -1)
+    cross_down = shift(-1, -1)
 
     def normalize_image(c, _):
         r = pl.ds(pl.multiple_of(c * SEND, SEND), SEND)
@@ -95,27 +97,35 @@
         iu[r, :] = (v * inv).astype(BF16)
         return 0
 
-    lax.fori_loop(0, SENDS, normalize_image, 0)
+    def send_image(c, _):
+        r = pl.ds(pl.multiple_of(c * SEND, SEND), SEND)
+        start_copy(iu.at[r], images.at[0, r], is2.at[c], images_got.at[c], down)
+
+        @pl.when(direct_image)
+        def _():
+            start_copy(iu.at[r], images.at[1, r], is3.at[c], images_got.at[SENDS + c], cross_down)
+
+        return 0
+
+    def normalize_and_send(c, _):
+        normalize_image(c, 0)
+        return send_image(c, 0)
+
+    for load in loads[SENDS + 2 :]:
+        load.wait()
+    scale = scale_ref[0]
+    bias = bias_ref[0]
+    for c in range(ROWS // 128):
+        cols = pl.ds(c * 128, 128)
+        square = jnp.broadcast_to(index_ref[cols].reshape(1, 128), (128, 128))
+        idx[:, cols] = square[0:8]
+        idx_col[cols, :] = square.T
+    lax.fori_loop(0, 2, normalize_image, 0)
     pl.semaphore_wait(barrier, len(partners))
-
-    direct_image = jnp.logical_or(odd, z == 0)
-    direct_text = jnp.logical_or(even, z == 3)
-    down = shift(0, -1)
-    cross_down = shift(-1, -1)
-    start_copy(idx, idx2, xs2, xr2, down)
-    start_copy(idx, idx3, xs3, xr3, cross_down)
-
-    def send_images(c, _):
-        r = pl.ds(pl.multiple_of(c * SEND, SEND), SEND)
-        start_copy(iu.at[r], i2.at[r], is2.at[c], ir2.at[c], down)
-
-        @pl.when(direct_image)
-        def _():
-            start_copy(iu.at[r], i3.at[r], is3.at[c], ir3.at[c], cross_down)
-
-        return 0
-
-    lax.fori_loop(0, SENDS, send_images, 0)
+    start_copy(idx, far_idx.at[0], xs2, far_idx_got.at[0], down)
+    start_copy(idx, far_idx.at[1], xs3, far_idx_got.at[1], cross_down)
+    lax.fori_loop(0, 2, send_image, 0)
+    lax.fori_loop(2, SENDS, normalize_and_send, 0)
 
     loads[SENDS].wait()
     loads[SENDS + 1].wait()
@@ -141,21 +151,25 @@
     up = shift(0, 1)
     cross_up = shift(1, 1)
 
-    def send_texts(c, _):
-        r = pl.ds(pl.multiple_of(c * SEND, SEND), SEND)
-        start_copy(tu.at[r], t2.at[r], ts2.at[c], tr2.at[c], up)
-
-        @pl.when(direct_text)
-        def _():
+    def send_t2(first=0, last=SENDS):
+        def step(c, _):
+            r = pl.ds(pl.multiple_of(c * SEND, SEND), SEND)
+            start_copy(tu.at[r], t2.at[r], ts2.at[c], tr2.at[c], up)
+            return 0
+
+        lax.fori_loop(first, last, step, 0)
+
+    def send_t3():
+        def step(c, _):
+            r = pl.ds(pl.multiple_of(c * SEND, SEND), SEND)
             start_copy(tu.at[r], t3.at[r], ts3.at[c], tr3.at[c], cross_up)
-
-        return 0
-
-    lax.fori_loop(0, SENDS, send_texts, 0)
-
-    for c in range(ROWS // 128):
-        row = jnp.broadcast_to(index_ref[0:1, pl.ds(c * 128, 128)], (128, 128))
-        idx_col[pl.ds(c * 128, 128), :] = row.T
+            return 0
+
+        lax.fori_loop(0, SENDS, step, 0)
+
+    direct_text = jnp.logical_or(even, z == 3)
+    pl.when(even)(send_t2)
+    pl.when(jnp.logical_xor(odd, z != 3))(send_t3)
 
     own_first = (g * 16 + k) * ROWS
 
@@ -165,9 +179,9 @@
         s = 1.0 / (1.0 + jnp.exp(-v))
         return jnp.where(match, -s, s).astype(BF16)
 
-    def text_logits(c, images, index):
+    def text_logits(c, block, index):
         r = pl.ds(pl.multiple_of(c * TILE, TILE), TILE)
-        logits = lax.dot_general(tu[...], images[r, :], (((1,), (1,)), ((), ())), preferred_element_type=F32)
+        logits = lax.dot_general(tu[...], block[r, :], (((1,), (1,)), ((), ())), preferred_element_type=F32)
         match = (index[0:1, r] - own_first) == lax.broadcasted_iota(jnp.int32, (ROWS, TILE), 0)
         w[:, r] = weights(logits, match)
 
@@ -188,14 +202,17 @@
 
         lax.fori_loop(0, E // TILE, step, 0)
 
-    def text_side(images, index, first, before):
+    def text_weights(block, index, before):
         def step(c, _):
             before(c)
-            text_logits(c, images, index)
+            text_logits(c, block, index)
             return 0
 
         lax.fori_loop(0, TILES, step, 0)
-        add_grad(g_text, images, first)
+
+    def text_side(block, index, first, before):
+        text_weights(block, index, before)
+        add_grad(g_text, block, first)
 
     def image_side(texts, first_row, first, before):
         def step(c, _):
@@ -216,7 +233,7 @@
             for i in range(per):
                 m = c * per + i
                 r = pl.ds(pl.multiple_of(m * SEND, SEND), SEND)
-                wait_got(buffer.at[r], sems.at[m])
+                wait_got(buffer(r), sems(m))
                 forward(m, r)
 
         return before
@@ -226,16 +243,25 @@
 
     forward_image = jnp.logical_and(odd, z != 0)
     forward_text = jnp.logical_and(even, z != 3)
+    forward_early = jnp.logical_and(forward_text, z != 0)
+    forward_late = jnp.logical_and(even, z == 0)
 
     def pass_image(m, r):
         @pl.when(forward_image)
         def _():
-            start_copy(i2.at[r], i3.at[r], is3r.at[m], ir3.at[m], shift(-1, 0))
-
-    def pass_text(m, r):
-        @pl.when(forward_text)
-        def _():
+            start_copy(images.at[0, r], images.at[1, r], is3r.at[m], images_got.at[SENDS + m], shift(-1, 0))
+
+    def pass_text(c):
+        for i in range(per):
+            m = c * per + i
+            r = pl.ds(pl.multiple_of(m * SEND, SEND), SEND)
+            wait_got(t2.at[r], tr2.at[m])
             start_copy(t2.at[r], t3.at[r], ts3r.at[m], tr3.at[m], shift(1, 0))
+
+    first_t2 = (g * 16 + (k + 15) % 16) * ROWS
+
+    def image_t2(before):
+        image_side(t2, first_t2, False, before)
 
     text_side(iu, idx, True, nothing)
     image_side(tu, own_first, True, nothing)
@@ -248,27 +274,46 @@
 
     lax.fori_loop(0, FT // TILE, turn, 0)
 
-    wait_got(idx2, xr2)
-    text_side(i2, idx2, False, got(i2, ir2, pass_image))
-    before_t2 = got(t2, tr2, pass_text)
-
-    def step_t2(c, _):
-        before_t2(c)
-        return 0
-
-    lax.fori_loop(0, TILES, step_t2, 0)
-    wait_got(idx3, xr3)
-    text_side(i3, idx3, False, got(i3, ir3, no_forward))
+    late_row = jnp.logical_and(odd, z == 0)
+    one = jnp.where(late_row, 1, 0)
+    two = 1 - one
+    pl.when(late_row)(lambda: image_t2(got(lambda r: t2.at[r], lambda m: tr2.at[m], no_forward)))
+
+    @pl.when(jnp.logical_and(even, z == 3))
+    def _():
+        def step(c, _):
+            wait_sent(iu.at[pl.ds(pl.multiple_of(c * SEND, SEND), SEND)], is2.at[c])
+            return 0
+
+        lax.fori_loop(0, SENDS, step, 0)
+        send_t3()
+
+    def before_one(c):
+        @pl.when(jnp.logical_and(late_row, c == TILES - 1))
+        def _():
+            send_t2()
+
+        got(lambda r: images.at[one, r], lambda m: images_got.at[one * SENDS + m], pass_image)(c)
+
+        @pl.when(jnp.logical_and(jnp.logical_and(odd, z != 0), c == TILES - 1))
+        def _():
+            send_t2()
+
+    wait_got(far_idx.at[one], far_idx_got.at[one])
+    text_side(images.at[one], far_idx.at[one], False, before_one)
+    pl.when(jnp.logical_and(odd, z != 0))(lambda: image_t2(got(lambda r: t2.at[r], lambda m: tr2.at[m], no_forward)))
+    wait_got(far_idx.at[two], far_idx_got.at[two])
+    text_weights(images.at[two], far_idx.at[two], got(lambda r: images.at[two, r], lambda m: images_got.at[two * SENDS + m], no_forward))
 
     def finish_text(c, _):
-        r = pl.ds(pl.multiple_of(c * SEND, SEND), SEND)
+        r = pl.ds(pl.multiple_of(c * TILE, TILE), TILE)
         u = tu32[r, :]
-        v = g_text[r, :] * scale
+        v = (g_text[r, :] + jnp.dot(w[r, :], images[two], preferred_element_type=F32)) * scale
         dot = jnp.sum(u * v, axis=1, keepdims=True)
         gp[r, :] = ((v - u * dot) * trs[r, 0:1]).astype(BF16)
         return 0
 
-    lax.fori_loop(0, SENDS, finish_text, 0)
+    lax.fori_loop(0, TILES, finish_text, 0)
 
     r1 = (r1a, r1b, r1c)
     e_ = (e_a, e_b, e_c)
@@ -289,6 +334,23 @@
                 cap_t[rows, :], gp[:, pl.ds(pl.multiple_of(theirs + n * TILE, TILE), TILE)], preferred_element_type=F32
             ).astype(BF16)
         start_copy(hs.at[rows], r0.at[rows], s0s.at[p], s0r.at[p], other_core)
+
+    @pl.when(forward_early)
+    def _():
+        def step(c, _):
+            pass_text(c)
+            return 0
+
+        lax.fori_loop(0, TILES, step, 0)
+        image_t2(nothing)
+
+    @pl.when(forward_late)
+    def _():
+        def step(c, _):
+            pass_text(c)
+            return 0
+
+        lax.fori_loop(0, TILES - 1, step, 0)
 
     for p in range(3):
         base, own, order = PARTS[p]
@@ -309,13 +371,20 @@
                 r1[p].at[s - 1], rs_s.at[p, 0, s - 1], rs_r.at[p, 0, s - 1], on_axis(order[0], s),
             )
 
+    @pl.when(forward_late)
+    def _():
+        pass_text(TILES - 1)
+
+    def late_t2(c):
+        pl.when(z == 3)(lambda: got(lambda r: t2.at[r], lambda m: tr2.at[m], no_forward)(c))
+
+    pl.when(jnp.logical_and(even, jnp.logical_or(z == 0, z == 3)))(lambda: image_t2(late_t2))
+
     def total(own, parts):
         v = own.astype(F32)
         for s in range(3):
             v = v + parts[s].astype(F32)
         return v.astype(BF16)
-
-    image_side(t2, (g * 16 + (k + 15) % 16) * ROWS, False, nothing)
 
     for p in range(3):
         base, own, order = PARTS[p]
@@ -388,7 +457,7 @@
         ref = out_ref.at[block(p, a, None, None)]
         start_copy(ref, ref, a0s.at[p, 0], a0r.at[p, 0], other_core)
 
-    image_side(t3, (((g + 7) % 8) * 16 + (k + 15) % 16) * ROWS, False, got(t3, tr3, no_forward))
+    image_side(t3, (((g + 7) % 8) * 16 + (k + 15) % 16) * ROWS, False, got(lambda r: t3.at[r], lambda m: tr3.at[m], no_forward))
 
     def finish_image(c, _):
         r = pl.ds(pl.multiple_of(c * SEND, SEND), SEND)
@@ -420,9 +489,12 @@
 
     def drain(c, _):
         r = pl.ds(pl.multiple_of(c * SEND, SEND), SEND)
-        wait_sent(iu.at[r], is2.at[c])
         wait_sent(tu.at[r], ts2.at[c])
 
+        @pl.when(jnp.logical_or(odd, z != 3))
+        def _():
+            wait_sent(iu.at[r], is2.at[c])
+
         @pl.when(direct_image)
         def _():
             wait_sent(iu.at[r], is3.at[c])
@@ -433,7 +505,7 @@
 
         @pl.when(forward_image)
         def _():
-            wait_sent(i2.at[r], is3r.at[c])
+            wait_sent(images.at[0, r], is3r.at[c])
 
         @pl.when(forward_text)
         def _():
@@ -465,19 +537,31 @@
     index = vmem((8, ROWS), jnp.int32)
     owns = [own for _, own, _ in PARTS]
     return [
-        wide, vmem((ROWS, FT), BF16), vmem((FT, E), BF16), block, block, wide, vmem((ROWS, 128), F32), vmem((FT, ROWS), BF16),
-        block, block, block, block, index, index, index, vmem((ROWS, 128), jnp.int32),
+        pltpu.SMEM((1,), F32), pltpu.SMEM((1,), F32), vmem((ROWS,), jnp.int32), wide, vmem((ROWS, FT), BF16), vmem((FT, E), BF16), block, block, wide, vmem((ROWS, 128), F32), vmem((FT, ROWS), BF16),
+        vmem((2, ROWS, E), BF16), block, block, index, vmem((2, 8, ROWS), jnp.int32), vmem((ROWS, 128), jnp.int32),
         vmem((ROWS, ROWS), BF16), wide, wide, block, vmem((FT, HALF), BF16), vmem((FT, HALF), BF16), vmem((FT, HALF), BF16),
         *[vmem((3, 4 * own, HALF), BF16) for own in owns],
         *[vmem((4 * own, HALF), BF16) for own in owns],
         *[vmem((3, own, HALF), BF16) for own in owns],
         *[vmem((own, HALF), BF16) for own in owns],
         *[vmem((3, own, 128), BF16) for own in owns],
-        dma((SENDS + 2,)),
-        *[dma((SENDS,)) for _ in range(10)],
-        dma, dma, dma, dma,
+        dma((SENDS + 5,)),
+        *[dma((SENDS,)) for _ in range(3)], dma((2 * SENDS,)), *[dma((SENDS,)) for _ in range(5)],
+        dma, dma, dma((2,)),
         dma((3,)), dma((3,)), dma((3, 3, 3)), dma((3, 3, 3)), dma((3, 3, 3)), dma((3, 3, 3)), dma((3, 4)), dma((3, 4)),
     ]
+
+
+def widen(a_ref, b_ref, a_out, b_out, a_wide, b_wide, sem):
+    copies = []
+    for ref, out, wide, first in ((b_ref, b_out, b_wide, 0), (a_ref, a_out, a_wide, FT // TILE)):
+        for c in range(ref.shape[0] // TILE):
+            r = pl.ds(c * TILE, TILE)
+            wide[r, :] = ref[r, :].astype(F32)
+            copies.append(pltpu.make_async_copy(wide.at[r], out.at[r], sem.at[first + c]))
+            copies[-1].start()
+    for copy in copies:
+        copy.wait()
 
 
 def on_device(
@@ -488,23 +572,31 @@
     similarity_scaling,
     score_offset,
 ):
-    smem = pl.BlockSpec(memory_space=pltpu.SMEM)
     vmem = pl.BlockSpec(memory_space=pltpu.VMEM)
     anywhere = pl.BlockSpec(memory_space=pl.ANY)
     grad_image, grad_proj = pl.pallas_call(
         kernel,
         out_shape=(jax.ShapeDtypeStruct((ROWS, E), BF16), jax.ShapeDtypeStruct((FT, E), BF16)),
-        in_specs=[smem, smem, vmem, anywhere, anywhere, anywhere],
+        in_specs=[pl.BlockSpec(memory_space=pltpu.HBM)] * 6,
         out_specs=(vmem, vmem),
         scratch_shapes=scratch(),
         compiler_params=pltpu.CompilerParams(
-            collective_id=0, has_side_effects=True, vmem_limit_bytes=52 * 1024 * 1024
+            collective_id=0, has_side_effects=True, vmem_limit_bytes=48 * 1024 * 1024
         ),
     )(
-        similarity_scaling, score_offset, matching_caption_index.reshape(1, ROWS),
+        similarity_scaling, score_offset, matching_caption_index,
         picture_embedding_unscaled, caption_tower_outputs, caption_mapping_matrix,
     )
-    return grad_image.astype(F32), grad_proj.astype(F32)
+    return pl.pallas_call(
+        widen,
+        out_shape=(jax.ShapeDtypeStruct((ROWS, E), F32), jax.ShapeDtypeStruct((FT, E), F32)),
+        in_specs=[vmem, vmem],
+        out_specs=(anywhere, anywhere),
+        scratch_shapes=[
+            pltpu.VMEM((ROWS, E), F32), pltpu.VMEM((FT, E), F32), pltpu.SemaphoreType.DMA(((ROWS + FT) // TILE,)),
+        ],
+        compiler_params=pltpu.CompilerParams(vmem_limit_bytes=16 * 1024 * 1024),
+    )(grad_image, grad_proj)
 
 
 def solution(mesh):

time: 117 us -> 106 us (0.906)
  Pallas kernels: 108 us -> 101 us
  other arithmetic: 6.82 us -> 0 us
  local copies, waits for them, and re-layouts: 0.69 us -> 2.22 us
    pallas_call x1, Pallas kernels: 108 us -> 98 us  [on_device(): pl.pallas_call(kernel, out_shape=(jax.ShapeDtypeStruct((ROWS, E), BF16),...]
    convert_element_type x2 -> x0, other arithmetic: 6.82 us -> none  [on_device(): return (grad_image.astype(F32), grad_proj.astype(F32))]
    pallas_call x0 -> x1, Pallas kernels: none -> 3.44 us  [on_device(): pl.pallas_call(widen, out_shape=(jax.ShapeDtypeStruct((ROWS, E), F32), ja...]
    unnamed x0 -> x4, local copies, waits for them, and re-layouts: none -> 2.22 us
where the time goes in v2:
time: 106 us
  Pallas kernels  101 us (95%)
  local copies, waits for them, and re-layouts  2.22 us (2%)
  between operations  2.1 us (2%)
    pallas_call x1, Pallas kernels, on_device(): pl.pallas_call(kernel, out_shape=(jax.ShapeDtypeStruct((ROWS, E), BF16),...  98 us
    pallas_call x1, Pallas kernels, on_device(): pl.pallas_call(widen, out_shape=(jax.ShapeDtypeStruct((ROWS, E), F32), ja...  3.44 us
    unnamed x4, local copies, waits for them, and re-layouts  2.22 us

profile of v2, /device:TPU:1, one launch (start us, length us, event | category | flops | bytes accessed | tf_op | source)
XLA Modules:
  0.0 105.7 jit_solution(16637578310355727350)
XLA Ops:
  1.9 0.0 copy-start
  1.9 1.5 %copy-done = bf16[768,1280]{1,0:T(8,128)(2,1)S(1)} copy-done((bf16[768,1280]{1,0:T(8,128)(2,1)S(1)}, bf16[768,1280]{1,0:T(8,128)(2,1)}, u32[]{:S(2)}) %copy-start) | copy-done | bytes 1966104
  3.5 0.0 copy-start.1
  3.5 0.7 copy-done.1
  4.2 98.0 %shard_map.77 = (bf16[768,1024]{1,0:T(8,128)(2,1)S(1)}, bf16[1280,1024]{1,0:T(8,128)(2,1)S(1)}) custom-call(f32[1]{0:T(128)S(6)} %copy.8.scale_hbm, f32[1]{0:T(128)S(6)} %copy.9.bias_hbm, s32[768]{0:T(1024)S(1)} %copy-done.1, f32[768,1024]{1,0:T(8,128)} %pic_hbm.1, bf16[768,1280]{1,0:T(8,128)(2,1)S(1)} %copy-done, bf16[1280,1024]{1,0:T(8,128)(2,1)} %head_hbm.1), custom_call_target="tpu_custom_call" | custom-call | tf_op jit(solution)/shard_map/pallas_call | solution.py:577
  102.1 3.4 %shard_map.78 = (f32[768,1024]{1,0:T(8,128)}, f32[1280,1024]{1,0:T(8,128)}) custom-call(bf16[768,1024]{1,0:T(8,128)(2,1)S(1)} %get-tuple-element.4.a_ref, bf16[1280,1024]{1,0:T(8,128)(2,1)S(1)} %get-tuple-element.5.b_ref), custom_call_target="tpu_custom_call" | custom-call | tf_op jit(solution)/shard_map/pallas_call | solution.py:590
Async XLA Ops:
  1.9 1.5 %copy-start = (bf16[768,1280]{1,0:T(8,128)(2,1)S(1)}, bf16[768,1280]{1,0:T(8,128)(2,1)}, u32[]{:S(2)}) copy-start(bf16[768,1280]{1,0:T(8,128)(2,1)} %cap_hbm.1) | copy-start | bytes 5898244
  3.5 0.7 copy-start.1

commit v3 on v2

--- a/solution.py
+++ b/solution.py
@@ -13,12 +13,14 @@
 SENDS = ROWS // SEND
 TILE = 256
 TILES = ROWS // TILE
+LAST = ROWS - TILE
 HALF = E // 2
+DETOUR = 2
 MESH = pl.DeviceIdType.MESH
 BF16 = jnp.bfloat16
 F32 = jnp.float32
 
-PARTS = ((0, 32, "yzx"), (512, 32, "zyx"), (1024, 16, "xyz"))
+PARTS = ((0, 32, "zyx"), (512, 32, "yzx"), (1024, 16, "xyz"))
 
 
 def start_copy(src, dst, send, recv, device):
@@ -38,9 +40,9 @@
 def kernel(
     scale_hbm, bias_hbm, index_hbm, pic_hbm, cap_hbm, head_hbm,
     gi_ref, out_ref,
-    scale_ref, bias_ref, index_ref, pic, cap, head, iu, tu, tu32, trs, cap_t, images, t2, t3, idx, far_idx, idx_col,
+    scale_ref, bias_ref, index_ref, pic, cap, head, iu, tu, tu32, trs, cap_t, images, t2, t3, tx, idx, far_idx, idx_col,
     w, g_text, g_image, gp, hs, r0, d, r1a, r1b, r1c, e_a, e_b, e_c, r2a, r2b, r2c, f_a, f_b, f_c, r3a, r3b, r3c,
-    load_sem, is2, is3, is3r, images_got, ts2, tr2, ts3, tr3, ts3r, xs2, xs3, far_idx_got,
+    load_sem, is2, is3, is3r, images_got, ts2, tr2, ts3, tr3, ts3r, txs, txr, txf, xs2, xs3, far_idx_got,
     s0s, s0r, rs_s, rs_r, ag_s, ag_r, a0s, a0r,
 ):
     g = lax.axis_index("group")
@@ -86,6 +88,8 @@
         pl.semaphore_signal(barrier, inc=1, device_id=p, device_id_type=MESH)
 
     direct_image = jnp.logical_or(odd, z == 0)
+    late_row = jnp.logical_and(odd, z == 0)
+    hand_on = jnp.logical_and(odd, z == 1)
     down = shift(0, -1)
     cross_down = shift(-1, -1)
 
@@ -171,6 +175,15 @@
     pl.when(even)(send_t2)
     pl.when(jnp.logical_xor(odd, z != 3))(send_t3)
 
+    @pl.when(late_row)
+    def _():
+        def step(c, _):
+            r = pl.ds(pl.multiple_of(c * SEND, SEND), SEND)
+            start_copy(tu.at[r], tx.at[r], txs.at[c], txr.at[c], shift(1, 0))
+            return 0
+
+        lax.fori_loop(0, DETOUR * (TILE // SEND), step, 0)
+
     own_first = (g * 16 + k) * ROWS
 
     def weights(logits, match):
@@ -242,9 +255,7 @@
         pass
 
     forward_image = jnp.logical_and(odd, z != 0)
-    forward_text = jnp.logical_and(even, z != 3)
-    forward_early = jnp.logical_and(forward_text, z != 0)
-    forward_late = jnp.logical_and(even, z == 0)
+    forward_text = jnp.logical_and(even, jnp.logical_and(z != 0, z != 3))
 
     def pass_image(m, r):
         @pl.when(forward_image)
@@ -274,7 +285,6 @@
 
     lax.fori_loop(0, FT // TILE, turn, 0)
 
-    late_row = jnp.logical_and(odd, z == 0)
     one = jnp.where(late_row, 1, 0)
     two = 1 - one
     pl.when(late_row)(lambda: image_t2(got(lambda r: t2.at[r], lambda m: tr2.at[m], no_forward)))
@@ -289,9 +299,9 @@
         send_t3()
 
     def before_one(c):
-        @pl.when(jnp.logical_and(late_row, c == TILES - 1))
-        def _():
-            send_t2()
+        @pl.when(jnp.logical_and(late_row, c == 1))
+        def _():
+            send_t2(DETOUR * per)
 
         got(lambda r: images.at[one, r], lambda m: images_got.at[one * SENDS + m], pass_image)(c)
 
@@ -303,12 +313,39 @@
     text_side(images.at[one], far_idx.at[one], False, before_one)
     pl.when(jnp.logical_and(odd, z != 0))(lambda: image_t2(got(lambda r: t2.at[r], lambda m: tr2.at[m], no_forward)))
     wait_got(far_idx.at[two], far_idx_got.at[two])
-    text_weights(images.at[two], far_idx.at[two], got(lambda r: images.at[two, r], lambda m: images_got.at[two * SENDS + m], no_forward))
+
+    def before_two(c):
+        got(lambda r: images.at[two, r], lambda m: images_got.at[two * SENDS + m], no_forward)(c)
+
+        @pl.when(jnp.logical_and(hand_on, c < DETOUR))
+        def _():
+            for i in range(per):
+                m = c * per + i
+                r = pl.ds(pl.multiple_of(m * SEND, SEND), SEND)
+                wait_got(tx.at[r], txr.at[m])
+                start_copy(tx.at[r], t3.at[r], txf.at[m], tr3.at[m], shift(0, 1))
+
+    def step_two(c, _):
+        before_two(c)
+        text_logits(c, images.at[two], far_idx.at[two])
+
+        @pl.when(c == TILES - 2)
+        def _():
+            def add(n, _):
+                cols = pl.ds(pl.multiple_of(n * TILE, TILE), TILE)
+                g_text[:, cols] += jnp.dot(w[:, 0:LAST], images[two, 0:LAST, cols], preferred_element_type=F32)
+                return 0
+
+            lax.fori_loop(0, E // TILE, add, 0)
+
+        return 0
+
+    lax.fori_loop(0, TILES, step_two, 0)
 
     def finish_text(c, _):
         r = pl.ds(pl.multiple_of(c * TILE, TILE), TILE)
         u = tu32[r, :]
-        v = (g_text[r, :] + jnp.dot(w[r, :], images[two], preferred_element_type=F32)) * scale
+        v = (g_text[r, :] + jnp.dot(w[r, LAST:], images[two, LAST:], preferred_element_type=F32)) * scale
         dot = jnp.sum(u * v, axis=1, keepdims=True)
         gp[r, :] = ((v - u * dot) * trs[r, 0:1]).astype(BF16)
         return 0
@@ -335,22 +372,20 @@
             ).astype(BF16)
         start_copy(hs.at[rows], r0.at[rows], s0s.at[p], s0r.at[p], other_core)
 
-    @pl.when(forward_early)
+    @pl.when(forward_text)
     def _():
         def step(c, _):
             pass_text(c)
             return 0
 
         lax.fori_loop(0, TILES, step, 0)
-        image_t2(nothing)
-
-    @pl.when(forward_late)
+
+    first_even = jnp.logical_and(even, z == 0)
+
+    @pl.when(first_even)
     def _():
-        def step(c, _):
+        for c in range(DETOUR, TILES):
             pass_text(c)
-            return 0
-
-        lax.fori_loop(0, TILES - 1, step, 0)
 
     for p in range(3):
         base, own, order = PARTS[p]
@@ -371,14 +406,27 @@
                 r1[p].at[s - 1], rs_s.at[p, 0, s - 1], rs_r.at[p, 0, s - 1], on_axis(order[0], s),
             )
 
-    @pl.when(forward_late)
+    def late_t2(c):
+        pl.when(jnp.logical_not(forward_text))(lambda: got(lambda r: t2.at[r], lambda m: tr2.at[m], no_forward)(c))
+
+    hand_down = jnp.logical_and(even, z == 1)
+
+    @pl.when(hand_down)
     def _():
-        pass_text(TILES - 1)
-
-    def late_t2(c):
-        pl.when(z == 3)(lambda: got(lambda r: t2.at[r], lambda m: tr2.at[m], no_forward)(c))
-
-    pl.when(jnp.logical_and(even, jnp.logical_or(z == 0, z == 3)))(lambda: image_t2(late_t2))
+        def step(m, _):
+            r = pl.ds(pl.multiple_of(m * SEND, SEND), SEND)
+            wait_got(t3.at[r], tr3.at[m])
+            start_copy(t3.at[r], t2.at[r], txf.at[m], tr2.at[m], shift(-1, 0))
+            return 0
+
+        lax.fori_loop(0, DETOUR * per, step, 0)
+
+    pl.when(jnp.logical_and(even, z != 0))(lambda: image_t2(late_t2))
+
+    @pl.when(first_even)
+    def _():
+        for c in range(DETOUR, TILES):
+            image_logits(c, t2, first_t2)
 
     def total(own, parts):
         v = own.astype(F32)
@@ -399,6 +447,16 @@
                 e_[p].at[pl.ds(pl.multiple_of(j * own, 16), own)],
                 r2[p].at[s - 1], rs_s.at[p, 1, s - 1], rs_r.at[p, 1, s - 1], on_axis(order[1], s),
             )
+
+    @pl.when(first_even)
+    def _():
+        def step(c, _):
+            got(lambda r: t2.at[r], lambda m: tr2.at[m], no_forward)(c)
+            image_logits(c, t2, first_t2)
+            return 0
+
+        lax.fori_loop(0, DETOUR, step, 0)
+
     for p in range(3):
         base, own, order = PARTS[p]
         for s in range(3):
@@ -412,6 +470,16 @@
                 f_[p].at[:, pl.ds(pl.multiple_of(j * 128, 128), 128)],
                 r3[p].at[s - 1], rs_s.at[p, 2, s - 1], rs_r.at[p, 2, s - 1], on_axis(order[2], s),
             )
+
+    def image_t3(c):
+        if c < DETOUR:
+            pl.when(jnp.logical_not(hand_down))(lambda: got(lambda r: t3.at[r], lambda m: tr3.at[m], no_forward)(c))
+        else:
+            got(lambda r: t3.at[r], lambda m: tr3.at[m], no_forward)(c)
+        image_logits(c, t3, (((g + 7) % 8) * 16 + (k + 15) % 16) * ROWS)
+
+    pl.when(first_even)(lambda: add_grad(g_image, t2, False))
+    pl.when(jnp.logical_not(first_even))(lambda: image_t3(0))
 
     def block(p, a, b, c):
         base, own, _ = PARTS[p]
@@ -444,11 +512,14 @@
         rows, cols = block(p, a, b, c)
         out_ref[rows, cols] = total(f_[p][:, pl.ds(pl.multiple_of(c * 128, 128), 128)], [r3[p][s] for s in range(3)])
         gather(p, 2, rows, cols)
+    pl.when(first_even)(lambda: image_t3(0))
+    image_t3(1)
     for p in range(3):
         a, b, c = seat(p)
         for s in (1, 2, 3):
             wait_got(out_ref.at[block(p, a, b, (c - s + 4) % 4)], ag_r.at[p, 2, s - 1])
         gather(p, 1, *block(p, a, b, None))
+    image_t3(2)
     for p in range(3):
         a, b, c = seat(p)
         for s in (1, 2, 3):
@@ -457,7 +528,7 @@
         ref = out_ref.at[block(p, a, None, None)]
         start_copy(ref, ref, a0s.at[p, 0], a0r.at[p, 0], other_core)
 
-    image_side(t3, (((g + 7) % 8) * 16 + (k + 15) % 16) * ROWS, False, got(lambda r: t3.at[r], lambda m: tr3.at[m], no_forward))
+    add_grad(g_image, t3, False)
 
     def finish_image(c, _):
         r = pl.ds(pl.multiple_of(c * SEND, SEND), SEND)
@@ -489,7 +560,9 @@
 
     def drain(c, _):
         r = pl.ds(pl.multiple_of(c * SEND, SEND), SEND)
-        wait_sent(tu.at[r], ts2.at[c])
+        @pl.when(jnp.logical_not(jnp.logical_and(late_row, c < DETOUR * per)))
+        def _():
+            wait_sent(tu.at[r], ts2.at[c])
 
         @pl.when(jnp.logical_or(odd, z != 3))
         def _():
@@ -507,9 +580,17 @@
         def _():
             wait_sent(images.at[0, r], is3r.at[c])
 
-        @pl.when(forward_text)
+        @pl.when(jnp.logical_or(forward_text, jnp.logical_and(first_even, c >= DETOUR * per)))
         def _():
             wait_sent(t2.at[r], ts3r.at[c])
+
+        @pl.when(jnp.logical_and(late_row, c < DETOUR * per))
+        def _():
+            wait_sent(tu.at[r], txs.at[c])
+
+        @pl.when(jnp.logical_and(z == 1, c < DETOUR * per))
+        def _():
+            wait_sent(tx.at[r], txf.at[c])
 
         return 0
 
@@ -538,7 +619,7 @@
     owns = [own for _, own, _ in PARTS]
     return [
         pltpu.SMEM((1,), F32), pltpu.SMEM((1,), F32), vmem((ROWS,), jnp.int32), wide, vmem((ROWS, FT), BF16), vmem((FT, E), BF16), block, block, wide, vmem((ROWS, 128), F32), vmem((FT, ROWS), BF16),
-        vmem((2, ROWS, E), BF16), block, block, index, vmem((2, 8, ROWS), jnp.int32), vmem((ROWS, 128), jnp.int32),
+        vmem((2, ROWS, E), BF16), block, block, block, index, vmem((2, 8, ROWS), jnp.int32), vmem((ROWS, 128), jnp.int32),
         vmem((ROWS, ROWS), BF16), wide, wide, block, vmem((FT, HALF), BF16), vmem((FT, HALF), BF16), vmem((FT, HALF), BF16),
         *[vmem((3, 4 * own, HALF), BF16) for own in owns],
         *[vmem((4 * own, HALF), BF16) for own in owns],
@@ -546,7 +627,7 @@
         *[vmem((own, HALF), BF16) for own in owns],
         *[vmem((3, own, 128), BF16) for own in owns],
         dma((SENDS + 5,)),
-        *[dma((SENDS,)) for _ in range(3)], dma((2 * SENDS,)), *[dma((SENDS,)) for _ in range(5)],
+        *[dma((SENDS,)) for _ in range(3)], dma((2 * SENDS,)), *[dma((SENDS,)) for _ in range(8)],
         dma, dma, dma((2,)),
         dma((3,)), dma((3,)), dma((3, 3, 3)), dma((3, 3, 3)), dma((3, 3, 3)), dma((3, 3, 3)), dma((3, 4)), dma((3, 4)),
     ]

time: 106 us -> 101 us (0.953)
  Pallas kernels: 101 us -> 97 us
    pallas_call x1, Pallas kernels: 98 us -> 93.5 us  [on_device(): pl.pallas_call(kernel, out_shape=(jax.ShapeDtypeStruct((ROWS, E), BF16),...]
where the time goes in v3:
time: 101 us
  Pallas kernels  97 us (96%)
  local copies, waits for them, and re-layouts  2.22 us (2%)
  between operations  2.1 us (2%)
    pallas_call x1, Pallas kernels, on_device(): pl.pallas_call(kernel, out_shape=(jax.ShapeDtypeStruct((ROWS, E), BF16),...  93.5 us
    pallas_call x1, Pallas kernels, on_device(): pl.pallas_call(widen, out_shape=(jax.ShapeDtypeStruct((ROWS, E), F32), ja...  3.44 us
    unnamed x4, local copies, waits for them, and re-layouts  2.22 us

profile of v3, /device:TPU:1, one launch (start us, length us, event | category | flops | bytes accessed | tf_op | source)
XLA Modules:
  0.0 101.3 jit_solution(15635030068706944432)
XLA Ops:
  1.9 0.0 copy-start
  1.9 1.5 %copy-done = bf16[768,1280]{1,0:T(8,128)(2,1)S(1)} copy-done((bf16[768,1280]{1,0:T(8,128)(2,1)S(1)}, bf16[768,1280]{1,0:T(8,128)(2,1)}, u32[]{:S(2)}) %copy-start) | copy-done | bytes 1966104
  3.5 0.0 copy-start.1
  3.5 0.7 copy-done.1
  4.2 93.5 %shard_map.77 = (bf16[768,1024]{1,0:T(8,128)(2,1)S(1)}, bf16[1280,1024]{1,0:T(8,128)(2,1)S(1)}) custom-call(f32[1]{0:T(128)S(6)} %copy.8.scale_hbm, f32[1]{0:T(128)S(6)} %copy.9.bias_hbm, s32[768]{0:T(1024)S(1)} %copy-done.1, f32[768,1024]{1,0:T(8,128)} %pic_hbm.1, bf16[768,1280]{1,0:T(8,128)(2,1)S(1)} %copy-done, bf16[1280,1024]{1,0:T(8,128)(2,1)} %head_hbm.1), custom_call_target="tpu_custom_call" | custom-call | tf_op jit(solution)/shard_map/pallas_call | solution.py:658
  97.7 3.4 %shard_map.78 = (f32[768,1024]{1,0:T(8,128)}, f32[1280,1024]{1,0:T(8,128)}) custom-call(bf16[768,1024]{1,0:T(8,128)(2,1)S(1)} %get-tuple-element.4.a_ref, bf16[1280,1024]{1,0:T(8,128)(2,1)S(1)} %get-tuple-element.5.b_ref), custom_call_target="tpu_custom_call" | custom-call | tf_op jit(solution)/shard_map/pallas_call | solution.py:671
Async XLA Ops:
  1.9 1.5 %copy-start = (bf16[768,1280]{1,0:T(8,128)(2,1)S(1)}, bf16[768,1280]{1,0:T(8,128)(2,1)}, u32[]{:S(2)}) copy-start(bf16[768,1280]{1,0:T(8,128)(2,1)} %cap_hbm.1) | copy-start | bytes 5898244
  3.5 0.7 copy-start.1

commit v4 on v3

--- a/solution.py
+++ b/solution.py
@@ -16,6 +16,7 @@
 LAST = ROWS - TILE
 HALF = E // 2
 DETOUR = 2
+DETOUR_BACK = 1
 MESH = pl.DeviceIdType.MESH
 BF16 = jnp.bfloat16
 F32 = jnp.float32
@@ -41,7 +42,7 @@
     scale_hbm, bias_hbm, index_hbm, pic_hbm, cap_hbm, head_hbm,
     gi_ref, out_ref,
     scale_ref, bias_ref, index_ref, pic, cap, head, iu, tu, tu32, trs, cap_t, images, t2, t3, tx, idx, far_idx, idx_col,
-    w, g_text, g_image, gp, hs, r0, d, r1a, r1b, r1c, e_a, e_b, e_c, r2a, r2b, r2c, f_a, f_b, f_c, r3a, r3b, r3c,
+    w, g_text, g_image, gp, hs, r0, d, r1a, r1b, r1c, e_a, e_b, e_c, r2a, r2b, r2c, r3a, r3b, r3c,
     load_sem, is2, is3, is3r, images_got, ts2, tr2, ts3, tr3, ts3r, txs, txr, txf, xs2, xs3, far_idx_got,
     s0s, s0r, rs_s, rs_r, ag_s, ag_r, a0s, a0r,
 ):
@@ -90,6 +91,8 @@
     direct_image = jnp.logical_or(odd, z == 0)
     late_row = jnp.logical_and(odd, z == 0)
     hand_on = jnp.logical_and(odd, z == 1)
+    last_odd = jnp.logical_and(odd, z == 3)
+    hand_back = jnp.logical_and(odd, z == 2)
     down = shift(0, -1)
     cross_down = shift(-1, -1)
 
@@ -305,9 +308,19 @@
 
         got(lambda r: images.at[one, r], lambda m: images_got.at[one * SENDS + m], pass_image)(c)
 
-        @pl.when(jnp.logical_and(jnp.logical_and(odd, z != 0), c == TILES - 1))
+        @pl.when(jnp.logical_and(jnp.logical_and(odd, jnp.logical_and(z != 0, z != 3)), c == TILES - 1))
         def _():
             send_t2()
+
+        @pl.when(jnp.logical_and(last_odd, c == TILES - 1))
+        def _():
+            def step(m, _):
+                r = pl.ds(pl.multiple_of(m * SEND, SEND), SEND)
+                start_copy(tu.at[r], tx.at[r], txs.at[m], txr.at[m], shift(-1, 0))
+                return 0
+
+            send_t2(DETOUR_BACK * per)
+            lax.fori_loop(0, DETOUR_BACK * per, step, 0)
 
     wait_got(far_idx.at[one], far_idx_got.at[one])
     text_side(images.at[one], far_idx.at[one], False, before_one)
@@ -355,7 +368,6 @@
     r1 = (r1a, r1b, r1c)
     e_ = (e_a, e_b, e_c)
     r2 = (r2a, r2b, r2c)
-    f_ = (f_a, f_b, f_c)
     r3 = (r3a, r3b, r3c)
     mine = pl.multiple_of(core * HALF, HALF)
     theirs = pl.multiple_of((1 - core) * HALF, HALF)
@@ -406,8 +418,22 @@
                 r1[p].at[s - 1], rs_s.at[p, 0, s - 1], rs_r.at[p, 0, s - 1], on_axis(order[0], s),
             )
 
-    def late_t2(c):
-        pl.when(jnp.logical_not(forward_text))(lambda: got(lambda r: t2.at[r], lambda m: tr2.at[m], no_forward)(c))
+    mid_even = jnp.logical_and(even, jnp.logical_or(z == 1, z == 2))
+    outer_even = jnp.logical_and(even, jnp.logical_or(z == 0, z == 3))
+    pl.when(mid_even)(lambda: image_t2(nothing))
+
+    def tile_t2(c):
+        got(lambda r: t2.at[r], lambda m: tr2.at[m], no_forward)(c)
+        image_logits(c, t2, first_t2)
+
+    @pl.when(outer_even)
+    def _():
+        def step(c, _):
+            pl.when(z == 3)(lambda: got(lambda r: t2.at[r], lambda m: tr2.at[m], no_forward)(c))
+            image_logits(c, t2, first_t2)
+            return 0
+
+        lax.fori_loop(jnp.where(z == 0, DETOUR, DETOUR_BACK), TILES, step, 0)
 
     hand_down = jnp.logical_and(even, z == 1)
 
@@ -421,12 +447,15 @@
 
         lax.fori_loop(0, DETOUR * per, step, 0)
 
-    pl.when(jnp.logical_and(even, z != 0))(lambda: image_t2(late_t2))
-
-    @pl.when(first_even)
+    @pl.when(hand_back)
     def _():
-        for c in range(DETOUR, TILES):
-            image_logits(c, t2, first_t2)
+        def step(m, _):
+            r = pl.ds(pl.multiple_of(m * SEND, SEND), SEND)
+            wait_got(tx.at[r], txr.at[m])
+            start_copy(tx.at[r], t2.at[r], txf.at[m], tr2.at[m], shift(1, 1))
+            return 0
+
+        lax.fori_loop(0, DETOUR_BACK * per, step, 0)
 
     def total(own, parts):
         v = own.astype(F32)
@@ -448,28 +477,25 @@
                 r2[p].at[s - 1], rs_s.at[p, 1, s - 1], rs_r.at[p, 1, s - 1], on_axis(order[1], s),
             )
 
-    @pl.when(first_even)
+    @pl.when(outer_even)
     def _():
         def step(c, _):
-            got(lambda r: t2.at[r], lambda m: tr2.at[m], no_forward)(c)
-            image_logits(c, t2, first_t2)
-            return 0
-
-        lax.fori_loop(0, DETOUR, step, 0)
+            tile_t2(c)
+            return 0
+
+        lax.fori_loop(0, jnp.where(z == 0, DETOUR, DETOUR_BACK), step, 0)
 
     for p in range(3):
         base, own, order = PARTS[p]
         for s in range(3):
             wait_got(r2[p].at[s], rs_r.at[p, 1, s])
         i = place[order[1]]
-        f_[p][...] = total(e_[p][pl.ds(pl.multiple_of(i * own, 16), own), :], [r2[p][s] for s in range(3)])
+        term = total(e_[p][pl.ds(pl.multiple_of(i * own, 16), own), :], [r2[p][s] for s in range(3)])
         i = place[order[2]]
+        r3[p][i] = term
         for s in (1, 2, 3):
-            j = (i + s) % 4
-            start_copy(
-                f_[p].at[:, pl.ds(pl.multiple_of(j * 128, 128), 128)],
-                r3[p].at[s - 1], rs_s.at[p, 2, s - 1], rs_r.at[p, 2, s - 1], on_axis(order[2], s),
-            )
+            ref = r3[p].at[i]
+            start_copy(ref, ref, rs_s.at[p, 2, s - 1], rs_r.at[p, 2, s - 1], on_axis(order[2], s))
 
     def image_t3(c):
         if c < DETOUR:
@@ -478,8 +504,8 @@
             got(lambda r: t3.at[r], lambda m: tr3.at[m], no_forward)(c)
         image_logits(c, t3, (((g + 7) % 8) * 16 + (k + 15) % 16) * ROWS)
 
-    pl.when(first_even)(lambda: add_grad(g_image, t2, False))
-    pl.when(jnp.logical_not(first_even))(lambda: image_t3(0))
+    pl.when(outer_even)(lambda: add_grad(g_image, t2, False))
+    pl.when(jnp.logical_not(outer_even))(lambda: image_t3(0))
 
     def block(p, a, b, c):
         base, own, _ = PARTS[p]
@@ -507,19 +533,13 @@
 
     for p in range(3):
         a, b, c = seat(p)
-        for s in range(3):
-            wait_got(r3[p].at[s], rs_r.at[p, 2, s])
-        rows, cols = block(p, a, b, c)
-        out_ref[rows, cols] = total(f_[p][:, pl.ds(pl.multiple_of(c * 128, 128), 128)], [r3[p][s] for s in range(3)])
-        gather(p, 2, rows, cols)
-    pl.when(first_even)(lambda: image_t3(0))
+        for s in (1, 2, 3):
+            wait_got(r3[p].at[(c - s + 4) % 4], rs_r.at[p, 2, s - 1])
+        rows, cols = block(p, a, b, None)
+        out_ref[rows, cols] = total(r3[p][0], [r3[p][s] for s in (1, 2, 3)])
+        gather(p, 1, rows, cols)
+    pl.when(outer_even)(lambda: image_t3(0))
     image_t3(1)
-    for p in range(3):
-        a, b, c = seat(p)
-        for s in (1, 2, 3):
-            wait_got(out_ref.at[block(p, a, b, (c - s + 4) % 4)], ag_r.at[p, 2, s - 1])
-        gather(p, 1, *block(p, a, b, None))
-    image_t3(2)
     for p in range(3):
         a, b, c = seat(p)
         for s in (1, 2, 3):
@@ -528,6 +548,7 @@
         ref = out_ref.at[block(p, a, None, None)]
         start_copy(ref, ref, a0s.at[p, 0], a0r.at[p, 0], other_core)
 
+    image_t3(2)
     add_grad(g_image, t3, False)
 
     def finish_image(c, _):
@@ -560,7 +581,14 @@
 
     def drain(c, _):
         r = pl.ds(pl.multiple_of(c * SEND, SEND), SEND)
-        @pl.when(jnp.logical_not(jnp.logical_and(late_row, c < DETOUR * per)))
+        away = jnp.logical_or(
+            jnp.logical_and(late_row, c < DETOUR * per), jnp.logical_and(last_odd, c < DETOUR_BACK * per)
+        )
+        handed = jnp.logical_or(
+            jnp.logical_and(z == 1, c < DETOUR * per), jnp.logical_and(hand_back, c < DETOUR_BACK * per)
+        )
+
+        @pl.when(jnp.logical_not(away))
         def _():
             wait_sent(tu.at[r], ts2.at[c])
 
@@ -584,11 +612,11 @@
         def _():
             wait_sent(t2.at[r], ts3r.at[c])
 
-        @pl.when(jnp.logical_and(late_row, c < DETOUR * per))
+        @pl.when(away)
         def _():
             wait_sent(tu.at[r], txs.at[c])
 
-        @pl.when(jnp.logical_and(z == 1, c < DETOUR * per))
+        @pl.when(handed)
         def _():
             wait_sent(tx.at[r], txf.at[c])
 
@@ -603,7 +631,6 @@
             wait_sent(r1[p].at[s], rs_s.at[p, 0, s])
             wait_sent(r2[p].at[s], rs_s.at[p, 1, s])
             wait_sent(r3[p].at[s], rs_s.at[p, 2, s])
-            wait_sent(out_ref.at[block(p, a, b, c)], ag_s.at[p, 2, s])
             wait_sent(out_ref.at[block(p, a, b, None)], ag_s.at[p, 1, s])
             wait_sent(out_ref.at[block(p, a, None, None)], ag_s.at[p, 0, s])
         for s in range(4):
@@ -624,8 +651,7 @@
         *[vmem((3, 4 * own, HALF), BF16) for own in owns],
         *[vmem((4 * own, HALF), BF16) for own in owns],
         *[vmem((3, own, HALF), BF16) for own in owns],
-        *[vmem((own, HALF), BF16) for own in owns],
-        *[vmem((3, own, 128), BF16) for own in owns],
+        *[vmem((4, own, HALF), BF16) for own in owns],
         dma((SENDS + 5,)),
         *[dma((SENDS,)) for _ in range(3)], dma((2 * SENDS,)), *[dma((SENDS,)) for _ in range(8)],
         dma, dma, dma((2,)),
@@ -665,8 +691,10 @@
             collective_id=0, has_side_effects=True, vmem_limit_bytes=48 * 1024 * 1024
         ),
     )(
-        similarity_scaling, score_offset, matching_caption_index,
-        picture_embedding_unscaled, caption_tower_outputs, caption_mapping_matrix,
+        similarity_scaling, score_offset,
+        *[pltpu.with_memory_space_constraint(a, pltpu.HBM) for a in (
+            matching_caption_index, picture_embedding_unscaled, caption_tower_outputs, caption_mapping_matrix,
+        )],
     )
     return pl.pallas_call(
         widen,

time: 101 us -> 95.6 us (0.947)
  Pallas kernels: 97 us -> 93.4 us
  local copies, waits for them, and re-layouts: 2.22 us -> 0 us
    pallas_call x1, Pallas kernels: 93.5 us -> 90 us  [on_device(): pl.pallas_call(kernel, out_shape=(jax.ShapeDtypeStruct((ROWS, E), BF16),...]
    unnamed x4 -> x0, local copies, waits for them, and re-layouts: 2.22 us -> none
where the time goes in v4:
time: 95.6 us; the launch traced here: 95.5 us
  Pallas kernels  93.4 us (98%)
  between operations  2.09 us (2%)
    pallas_call x1, Pallas kernels, on_device(): pl.pallas_call(kernel, out_shape=(jax.ShapeDtypeStruct((ROWS, E), BF16),...  90 us
    pallas_call x1, Pallas kernels, on_device(): pl.pallas_call(widen, out_shape=(jax.ShapeDtypeStruct((ROWS, E), F32), ja...  3.44 us

profile of v4, /device:TPU:1, one launch (start us, length us, event | category | flops | bytes accessed | tf_op | source)
XLA Modules:
  0.0 95.5 jit_solution(18108690353148616430)
XLA Ops:
  1.9 90.0 %shard_map.77 = (bf16[768,1024]{1,0:T(8,128)(2,1)S(1)}, bf16[1280,1024]{1,0:T(8,128)(2,1)S(1)}) custom-call(f32[1]{0:T(128)S(6)} %copy.8.scale_hbm, f32[1]{0:T(128)S(6)} %copy.9.bias_hbm, s32[768]{0:T(1024)} %index_hbm.1, f32[768,1024]{1,0:T(8,128)} %pic_hbm.1, bf16[768,1280]{1,0:T(8,128)(2,1)} %cap_hbm.1, bf16[1280,1024]{1,0:T(8,128)(2,1)} %head_hbm.1), custom_call_target="tpu_custom_call" | custom-call | tf_op jit(solution)/shard_map/pallas_call | solution.py:684
  91.9 3.4 %shard_map.78 = (f32[768,1024]{1,0:T(8,128)}, f32[1280,1024]{1,0:T(8,128)}) custom-call(bf16[768,1024]{1,0:T(8,128)(2,1)S(1)} %get-tuple-element.4.a_ref, bf16[1280,1024]{1,0:T(8,128)(2,1)S(1)} %get-tuple-element.5.b_ref), custom_call_target="tpu_custom_call" | custom-call | tf_op jit(solution)/shard_map/pallas_call | solution.py:699
